TPU v7x, 32 devices: a whole 2x2x4 slice. The times are simulated.
32 devices in a mesh: groups: 2 (over y), gx: 8 (over z, x), gy: 2 (over core).
Axes of the slice: x: 2, y: 2, z: 4, core: 2. Of those that a mesh axis runs over, the one named last changes fastest.
Arguments:
- residual: bfloat16 [128, 16384], P(('groups', 'gx'), 'gy'), parts along dimension 0, may hold values from -6 to 6
- query: bfloat16 [128, 16384], P('groups', ('gx', 'gy')), parts along dimension 0, may hold values from -6 to 6
- new_keyval: bfloat16 [128, 2048], P('groups', ('gx', 'gy')), parts along dimension 0, may hold values from -6 to 6
- key_cache: bfloat16 [128, 512, 1024], P(('groups', 'gx', 'gy')), parts along dimension 0, may hold values from -1000 to 1000
- value_cache: bfloat16 [128, 512, 1024], P(('groups', 'gx', 'gy')), parts along dimension 0, may hold values from -6 to 6
- lengths: int32 [128], P(('groups', 'gx', 'gy')), parts along dimension 0, may hold values from 1 to 511, as said below
- out_weight: bfloat16 [16384, 16384], P('gx', 'gy'), may hold values from -0.046875 to 0.046875
Outputs:
- layer_out: bfloat16 [128, 16384], P(('groups', 'gx'), 'gy'), parts along dimension 0
There are 2 independent parts, one for each index of `groups`. A program takes and returns all parts, laid end to end along the dimension named above; an argument that names none is the same for every part. Nothing has to cross between parts.
Inputs may be any that keep to these rules, and one draw needn't show every extreme that they name: Each request's new token takes position lengths[r]; positions 0 to lengths[r] are attended; one request has 511.
All inputs are finite; a program needn't handle non-finite values.
Results may differ from a plain program's by a relative error of at most 0.007.
The roundings to bfloat16 on the way count: a program that leaves them out, or rounds other values in their place, can miss the bound.
Values may be sent and summed in bfloat16 or wider, within the bound.
No kernel may reach another device: no remote copies, remote signals or barrier semaphores. Data moves between devices by JAX's collectives and lax.ppermute only.
A program may use at most 128 MiB of HBM per device.

v0:
```python
import math

import jax
import jax.numpy as jnp
from jax import lax
from jax.sharding import PartitionSpec as P

HEADS = 128
KV_HEADS = 8
HD = 128


rope_base = 500000.0


def sign_entries(row_index, col_index, matrix_order):
    anded = jnp.bitwise_and(row_index[:, None], col_index[None, :])
    parity = jnp.zeros(anded.shape, jnp.int32)
    for bit_index in range(int(matrix_order).bit_length()):
        parity = parity + jnp.bitwise_and(jnp.right_shift(anded, bit_index), 1)
    signs = 1.0 - 2.0 * jnp.bitwise_and(parity, 1).astype(jnp.float32)
    return signs / math.sqrt(matrix_order)


def sylvester(matrix_order):
    ladder = jnp.arange(matrix_order, dtype=jnp.int32)
    return sign_entries(ladder, ladder, matrix_order)


def rotary(vector, position):
    half_dim = vector.shape[-1] // 2
    frequency = rope_base ** (-2.0 * jnp.arange(half_dim, dtype=jnp.float32) / vector.shape[-1])
    angles = position[:, None] * frequency[None, :]
    angles = jnp.concatenate([angles, angles], axis=-1)[:, None, :]
    turned = jnp.concatenate([-vector[..., half_dim:], vector[..., :half_dim]], axis=-1)
    return vector * jnp.cos(angles) + turned * jnp.sin(angles)


def rotate_heads(vector, head_table):
    return jnp.einsum("rhd,de->rhe", vector, head_table, precision=lax.Precision.HIGHEST)


def mix_local(attended):
    mixing = sylvester(HEADS)
    mixed = jnp.einsum(
        "gh,rhd->rgd", mixing, attended.astype(jnp.float32), precision=lax.Precision.HIGHEST
    )
    return mixed.astype(jnp.bfloat16)


def shards(residual, query, new_keyval, key_cache, value_cache, lengths, out_weight):
    gx_count = lax.axis_size("gx")
    row_count = lengths.shape[0]
    max_slots = key_cache.shape[1]
    group_size = HEADS // KV_HEADS
    query_rows, keyval_rows = (
        lax.all_to_all(query, ("gx", "gy"), split_axis=0, concat_axis=1, tiled=True),
        lax.all_to_all(new_keyval, ("gx", "gy"), split_axis=0, concat_axis=1, tiled=True),
    )
    head_table = sylvester(HD)
    position = lengths.astype(jnp.float32)
    rope_query = rotate_heads(
        rotary(query_rows.astype(jnp.float32).reshape(row_count, HEADS, HD), position), head_table
    )
    rope_query = rope_query.astype(jnp.bfloat16)
    key_value = keyval_rows.reshape(row_count, 2, KV_HEADS, HD)
    new_key = rotate_heads(
        rotary(key_value[:, 0].astype(jnp.float32), position), head_table
    ).astype(jnp.bfloat16)
    new_value = key_value[:, 1]
    slot_index = jnp.arange(max_slots, dtype=jnp.int32)
    current = (slot_index[None, :] == lengths[:, None])[:, :, None, None]
    key_rows = jnp.where(
        current, new_key[:, None], key_cache.reshape(row_count, max_slots, KV_HEADS, HD)
    )
    value_rows = jnp.where(
        current, new_value[:, None], value_cache.reshape(row_count, max_slots, KV_HEADS, HD)
    )
    grouped = rope_query.reshape(row_count, KV_HEADS, group_size, HD)
    scores = jnp.einsum(
        "rkgd,rpkd->rkgp", grouped, key_rows, preferred_element_type=jnp.float32
    ) / math.sqrt(HD)
    visible = (slot_index[None, :] <= lengths[:, None])[:, None, None, :]
    scores = jnp.where(visible, scores, -jnp.inf)
    row_max = jnp.max(scores, axis=-1, keepdims=True)
    weights = jnp.exp(scores - row_max)
    weights = (weights / jnp.sum(weights, axis=-1, keepdims=True)).astype(jnp.bfloat16)
    attended = jnp.einsum(
        "rkgp,rpkd->rkgd", weights, value_rows, preferred_element_type=jnp.float32
    )
    attended = attended.astype(jnp.bfloat16).reshape(row_count, HEADS, HD)
    feature_width = HEADS * HD // gx_count
    head_major = mix_local(attended)
    pieces_in = lax.all_to_all(
        head_major.reshape(1, 1, row_count, gx_count, feature_width),
        "gx",
        split_axis=3,
        concat_axis=0,
        tiled=True,
    )
    gathered = lax.all_gather(pieces_in, "gy", axis=1, tiled=True)
    feature_rows = gathered.reshape(-1, feature_width)
    summed = lax.psum_scatter(
        jnp.dot(feature_rows, out_weight, preferred_element_type=jnp.float32),
        "gx",
        scatter_dimension=0,
        tiled=True,
    )
    return (residual.astype(jnp.float32) + summed).astype(jnp.bfloat16)


def solution(mesh):
    in_specs = (
        P(("groups", "gx"), "gy"),
        P("groups", ("gx", "gy")),
        P("groups", ("gx", "gy")),
        P(("groups", "gx", "gy"), None, None),
        P(("groups", "gx", "gy"), None, None),
        P(("groups", "gx", "gy")),
        P("gx", "gy"),
    )
    out_specs = P(("groups", "gx"), "gy")
    return jax.shard_map(shards, mesh=mesh, in_specs=in_specs, out_specs=out_specs, check_vma=False)
```

profile of v0, /device:TPU:0, one launch (start us, length us, event | category | flops | bytes accessed | tf_op | source)
XLA Modules:
  0.0 140.9 jit_solution(13148037798301461729)
XLA Ops:
  6.5 7.4 %all-to-all-start.1 = ((bf16[16,4,128]{2,1,0:T(4,128)(2,1)}), bf16[16,4,128]{2,1,0:T(4,128)(2,1)S(1)}, u32[]{:S(2)}, u32[]{:S(2)}) async-start(bf16[16,4,128]{2,1,0:T(4,128)(2,1)} %bitcast.65), calls=%async_computation.1 | async-start | bytes 32768 | tf_op jit(solution)/shard_map/all_to_all | solution.py:58
  13.9 0.7 convert_element_type.56
  14.6 0.7 iota_compare_fusion.1
  15.3 0.1 broadcast_multiply_fusion
  15.4 0.1 fusion.36
  15.5 1.6 %all_to_all.35 = bf16[16,4,1024]{2,1,0:T(4,128)(2,1)} reshape(bf16[64,1024]{1,0:T(8,128)(2,1)} %param.8) | data formatting | bytes 262144 | tf_op jit(solution)/shard_map/all_to_all | solution.py:57
  17.1 3.3 %all-to-all-done.1 = bf16[16,4,128]{2,1,0:T(4,128)(2,1)S(1)} async-done(((bf16[16,4,128]{2,1,0:T(4,128)(2,1)}), bf16[16,4,128]{2,1,0:T(4,128)(2,1)S(1)}, u32[]{:S(2)}, u32[]{:S(2)}) %all-to-all-start.1) | async-done | bytes 16416 | tf_op jit(solution)/shard_map/all_to_all | solution.py:58
  20.4 3.5 %all-to-all-start = ((bf16[16,4,1024]{2,1,0:T(4,128)(2,1)}), bf16[16,4,1024]{2,1,0:T(4,128)(2,1)S(1)}, u32[]{:S(2)}, u32[]{:S(2)}) async-start(bf16[16,4,1024]{2,1,0:T(4,128)(2,1)} %all_to_all.35), calls=%async_computation | async-start | bytes 262144 | tf_op jit(solution)/shard_map/all_to_all | solution.py:57
  23.9 0.0 reduce-scatter.2.cloned.1.call-start
  24.0 0.1 slice_negate_fusion.1
  24.1 0.2 convolution_convert_fusion.2
  24.3 7.5 %all-to-all-done = bf16[16,4,1024]{2,1,0:T(4,128)(2,1)S(1)} async-done(((bf16[16,4,1024]{2,1,0:T(4,128)(2,1)}), bf16[16,4,1024]{2,1,0:T(4,128)(2,1)S(1)}, u32[]{:S(2)}, u32[]{:S(2)}) %all-to-all-start) | async-done | bytes 131104 | tf_op jit(solution)/shard_map/all_to_all | solution.py:57
  31.8 0.2 copy.36
  32.1 0.1 slice_negate_fusion
  32.2 0.5 convolution_convert_fusion.1
  32.7 3.5 %fusion.72 = (f32[4,8,16]{2,1,0:T(8,128)S(1)}, f32[4,8,16,512]{3,2,1,0:T(8,128)S(1)}) fusion(bf16[4,8,16,128]{3,2,1,0:T(8,128)(2,1)S(1)} %bitcast.61, pred[4,512]{1,0:T(4,128)(4,1)S(1)} %get-tuple-element.14, bf16[4,8,128]{2,1,0:T(8,128)(2,1)S(1)} %convolution_convert_fusion.2, pred[4,512]{1,0:T(4,128)(4,1)S(1)} %get-tuple-element.13, ...), kind=kOutput, calls=%fused_computation.90 | convolution fusion | flops 70255104 | bytes 5388288 | tf_op jit(solution)/shard_map/sub | solution.py:86
  36.2 2.9 %fusion.13 = bf16[4,8,16,128]{3,2,1,0:T(8,128)(2,1)S(1)} fusion(pred[4,512]{1,0:T(4,128)(4,1)S(1)} %get-tuple-element.14, bf16[4,8,128]{2,1,0:T(8,128)(2,1)S(1)} %get-tuple-element.10, f32[4,8,16,512]{3,2,1,0:T(8,128)S(1)} %get-tuple-element.16, f32[4,8,16]{2,1,0:T(8,128)S(1)} %get-tuple-element.15, bf16[4,512,1024]{2,1,0:T(8,128)(2,1)} %param.11), kind=kOutput, calls=%fused_computation.17 | convolution fusion | flops 69795840 | bytes 5386240 | tf_op jit(solution)/shard_map/rkgp,rpkd->rkgd/dot_general | solution.py:88
  39.1 0.4 fusion.14
  39.5 0.1 copy.41
  39.6 0.1 reshape.136
  39.7 0.1 copy.42
  39.8 9.7 %all_to_all.47 = bf16[1,1,4,8,2048]{4,2,1,0,3:T(4,128)(2,1)S(1)} all-to-all(bf16[1,1,4,8,2048]{4,2,1,0,3:T(4,128)(2,1)S(1)} %copy.42), channel_id=1, replica_groups=mesh['groups'=2,'gx'=8,'gy'=2] {'gx'}, dimensions={3} | all-to-all | bytes 262144 | tf_op jit(solution)/shard_map/all_to_all | solution.py:94
  49.5 0.1 copy.43
  49.6 2.0 %all-gather = bf16[8,2,1,4,1,2048]{5,0,4,3,2,1:T(8,128)(2,1)S(1)} all-gather(bf16[8,1,1,4,1,2048]{5,0,4,3,2,1:T(8,128)(2,1)S(1)} %copy.43), channel_id=2, replica_groups=mesh['groups'=2,'gx'=8,'gy'=2] {'gy'}, dimensions={1}, use_global_device_ids=true | all-gather | bytes 393216 | tf_op jit(solution)/shard_map/all_gather | solution.py:101
  51.6 0.2 copy.44
  51.8 0.1 reshape.137
  51.9 0.0 copy-start
  51.9 14.9 %fusion.73 = f32[64,8192]{1,0:T(8,128)} fusion(bf16[64,2048]{1,0:T(8,128)(2,1)S(1)} %reshape.137, bf16[2048,8192]{1,0:T(8,128)(2,1)} %param.13), kind=kOutput, calls=%fused_computation.91 | convolution fusion | flops 2147483648 | bytes 35913728 | tf_op jit(solution)/shard_map/dot_general | solution.py:104
  66.8 0.0 reduce-scatter.2.cloned.1.call-update
  66.9 65.5 %reduce-scatter.2.cloned.1.call-done = f32[8,8192]{1,0:T(8,128)} async-done(((f32[64,8192]{1,0:T(8,128)}), f32[8,8192]{1,0:T(8,128)}) %reduce-scatter.2.cloned.1.call-update) | async-done | bytes 262160 | tf_op jit(solution)/shard_map/reduce_scatter | solution.py:103
  132.4 0.0 copy-done
  132.4 1.6 %add_convert_fusion = bf16[8,8192]{1,0:T(8,128)(2,1)} fusion(f32[8,8192]{1,0:T(8,128)} %reduce-scatter.2.cloned.1.call-done, bf16[8,8192]{1,0:T(8,128)(2,1)S(1)} %copy-done), kind=kLoop, calls=%fused_computation.28 | loop fusion | flops 196608 | bytes 524288 | tf_op jit(solution)/shard_map/convert_element_type | solution.py:109
  (5 shorter events, 0.1 us)
Async XLA Ops:
  6.5 13.9 %all-to-all-start.1 = ((bf16[16,4,128]{2,1,0:T(4,128)(2,1)}), bf16[16,4,128]{2,1,0:T(4,128)(2,1)S(1)}, u32[]{:S(2)}, u32[]{:S(2)}) async-start(bf16[16,4,128]{2,1,0:T(4,128)(2,1)} %bitcast.65), calls=%async_computation.1 | async-start | bytes 32768 | tf_op jit(solution)/shard_map/all_to_all | solution.py:58
  20.4 11.4 %all-to-all-start = ((bf16[16,4,1024]{2,1,0:T(4,128)(2,1)}), bf16[16,4,1024]{2,1,0:T(4,128)(2,1)S(1)}, u32[]{:S(2)}, u32[]{:S(2)}) async-start(bf16[16,4,1024]{2,1,0:T(4,128)(2,1)} %all_to_all.35), calls=%async_computation | async-start | bytes 262144 | tf_op jit(solution)/shard_map/all_to_all | solution.py:57
  23.9 108.5 %reduce-scatter.2.cloned.1.call-start = ((), (), s32[]{:S(2)}) async-start(), calls=%async_computation.4 | async-start | bytes 2359296 | tf_op jit(solution)/shard_map/reduce_scatter | solution.py:103
  51.9 80.5 %copy-start = (bf16[8,8192]{1,0:T(8,128)(2,1)S(1)}, bf16[8,8192]{1,0:T(8,128)(2,1)}, u32[]{:S(2)}) copy-start(bf16[8,8192]{1,0:T(8,128)(2,1)} %param.7) | copy-start | bytes 393220
Sparse Core Ops, SparseCore 0:
  67.0 65.3 reduce-scatter.1
where the time goes:
time: 141 us
  waiting for transfers between devices  76.4 us (54%)
  matrix products  22.4 us (16%)
  between operations  13.5 us (10%)
  blocking collectives  11.7 us (8%)
  starting transfers between devices  10.9 us (8%)
  other arithmetic  3.45 us (2%)
  local copies, waits for them, and re-layouts  2.48 us (2%)
    reduce_scatter x1, waiting for transfers between devices, shards(): lax.psum_scatter(jnp.dot(feature_rows, out_weight, preferred_element_type...  65.5 us
    dot_general x1, matrix products, shards(): jnp.dot(feature_rows, out_weight, preferred_element_type=jnp.float32)  14.9 us
    all_to_all x1, blocking collectives, shards(): lax.all_to_all(head_major.reshape(1, 1, row_count, gx_count, feature_widt...  9.74 us
    all_to_all x1, waiting for transfers between devices, shards(): lax.all_to_all(query, ('gx', 'gy'), split_axis=0, concat_axis=1, tiled=True)  7.52 us
    all_to_all x1, starting transfers between devices, shards(): lax.all_to_all(new_keyval, ('gx', 'gy'), split_axis=0, concat_axis=1, til...  7.36 us
    sub x1, matrix products, shards(): weights = jnp.exp(scores - row_max)  3.52 us
    all_to_all x1, starting transfers between devices, shards(): lax.all_to_all(query, ('gx', 'gy'), split_axis=0, concat_axis=1, tiled=True)  3.51 us
    all_to_all x1, waiting for transfers between devices, shards(): lax.all_to_all(new_keyval, ('gx', 'gy'), split_axis=0, concat_axis=1, til...  3.29 us
  transfers between devices with their start and end apart: 3, of which 3 were waited for; matrix products, arithmetic and copies ran while one was open for 1% of the time, Pallas kernels for 0%

commit v1 on v0

--- a/solution.py
+++ b/solution.py
@@ -53,10 +53,12 @@
     row_count = lengths.shape[0]
     max_slots = key_cache.shape[1]
     group_size = HEADS // KV_HEADS
-    query_rows, keyval_rows = (
-        lax.all_to_all(query, ("gx", "gy"), split_axis=0, concat_axis=1, tiled=True),
-        lax.all_to_all(new_keyval, ("gx", "gy"), split_axis=0, concat_axis=1, tiled=True),
-    )
+    query_width = query.shape[1]
+    fused_rows = jnp.concatenate([query, new_keyval], axis=1).reshape(-1, row_count, query_width + new_keyval.shape[1])
+    fused_rows = lax.all_to_all(fused_rows, ("gx", "gy"), split_axis=0, concat_axis=0, tiled=True)
+    fused_rows = fused_rows.transpose(1, 0, 2)
+    query_rows = fused_rows[:, :, :query_width].reshape(row_count, -1)
+    keyval_rows = fused_rows[:, :, query_width:].reshape(row_count, -1)
     head_table = sylvester(HD)
     position = lengths.astype(jnp.float32)
     rope_query = rotate_heads(
@@ -100,12 +102,10 @@
     )
     gathered = lax.all_gather(pieces_in, "gy", axis=1, tiled=True)
     feature_rows = gathered.reshape(-1, feature_width)
-    summed = lax.psum_scatter(
-        jnp.dot(feature_rows, out_weight, preferred_element_type=jnp.float32),
-        "gx",
-        scatter_dimension=0,
-        tiled=True,
-    )
+    partial = jnp.dot(feature_rows, out_weight, preferred_element_type=jnp.float32)
+    partial = partial.astype(jnp.bfloat16).reshape(gx_count, -1, out_weight.shape[1])
+    terms = lax.all_to_all(partial, "gx", split_axis=0, concat_axis=0, tiled=True)
+    summed = jnp.sum(terms.astype(jnp.float32), axis=0)
     return (residual.astype(jnp.float32) + summed).astype(jnp.bfloat16)
 
 

time: 141 us -> 81.2 us (0.58)
  waiting for transfers between devices: 76.4 us -> 6.6 us
  blocking collectives: 11.7 us -> 40.5 us
  between operations: 13.5 us -> 0.15 us
  starting transfers between devices: 10.9 us -> 7.36 us
    reduce_scatter x1 -> x0, waiting for transfers between devices: 65.5 us -> none  [shards(): lax.psum_scatter(jnp.dot(feature_rows, out_weight, preferred_element_type...]
    all_to_all x0 -> x1, blocking collectives: none -> 28.7 us  [shards(): lax.all_to_all(partial, 'gx', split_axis=0, concat_axis=0, tiled=True)]
    all_to_all x2 -> x1, waiting for transfers between devices: 10.8 us -> 6.6 us  [shards(): lax.all_to_all(fused_rows, ('gx', 'gy'), split_axis=0, concat_axis=0, til...]
    all_to_all x2 -> x1, starting transfers between devices: 10.9 us -> 7.36 us  [shards(): lax.all_to_all(fused_rows, ('gx', 'gy'), split_axis=0, concat_axis=0, til...]
    all_to_all x2 -> x1, local copies, waits for them, and re-layouts: 1.62 us -> 0.02 us  [shards(): lax.all_to_all(fused_rows, ('gx', 'gy'), split_axis=0, concat_axis=0, til...]
  transfers between devices with their start and end apart: 3 -> 1, of which waited for: 3 -> 1; matrix products, arithmetic and copies ran while one was open for 1% -> 2% of each run, Pallas kernels for 0% -> 0%
where the time goes in v1:
time: 81.2 us; the launch traced here: 80.8 us
  blocking collectives  40.5 us (50%)
  matrix products  21.2 us (26%)
  starting transfers between devices  7.36 us (9%)
  waiting for transfers between devices  6.6 us (8%)
  other arithmetic  3.6 us (4%)
  local copies, waits for them, and re-layouts  1.41 us (2%)
    all_to_all x1, blocking collectives, shards(): lax.all_to_all(partial, 'gx', split_axis=0, concat_axis=0, tiled=True)  28.7 us
    dot_general x1, matrix products, shards(): jnp.dot(feature_rows, out_weight, preferred_element_type=jnp.float32)  13.7 us
    all_to_all x1, blocking collectives, shards(): lax.all_to_all(head_major.reshape(1, 1, row_count, gx_count, feature_widt...  9.74 us
    all_to_all x1, starting transfers between devices, shards(): lax.all_to_all(fused_rows, ('gx', 'gy'), split_axis=0, concat_axis=0, til...  7.36 us
    all_to_all x1, waiting for transfers between devices, shards(): lax.all_to_all(fused_rows, ('gx', 'gy'), split_axis=0, concat_axis=0, til...  6.6 us
    sub x1, matrix products, shards(): weights = jnp.exp(scores - row_max)  3.52 us
    dot_general x1, matrix products, shards(): jnp.einsum('rkgp,rpkd->rkgd', weights, value_rows, preferred_element_type...  2.91 us
    all_gather x1, blocking collectives, shards(): gathered = lax.all_gather(pieces_in, 'gy', axis=1, tiled=True)  1.99 us
  transfers between devices with their start and end apart: 1, of which 1 were waited for; matrix products, arithmetic and copies ran while one was open for 2% of the time, Pallas kernels for 0%

profile of v1, /device:TPU:0, one launch (start us, length us, event | category | flops | bytes accessed | tf_op | source)
XLA Modules:
  0.0 80.8 jit_solution(2695581941719506130)
XLA Ops:
  0.0 0.9 %pad_maximum_fusion = bf16[64,1152]{1,0:T(8,128)(2,1)S(1)} fusion(bf16[64,128]{1,0:T(8,128)(2,1)} %param.9, bf16[64,1024]{1,0:T(8,128)(2,1)} %param.8), kind=kLoop, calls=%fused_computation.32 | loop fusion | flops 294912 | bytes 294912 | tf_op jit(solution)/shard_map/concatenate | solution.py:57
  0.9 0.7 reshape.128
  1.6 7.4 %all-to-all-start = ((bf16[16,4,1152]{2,1,0:T(4,128)(2,1)}), bf16[16,4,1152]{2,1,0:T(4,128)(2,1)S(1)}, u32[]{:S(2)}, u32[]{:S(2)}) async-start(bf16[16,4,1152]{2,1,0:T(4,128)(2,1)} %reshape.128), calls=%async_computation | async-start | bytes 294912 | tf_op jit(solution)/shard_map/all_to_all | solution.py:58
  9.0 0.7 convert_element_type.58
  9.7 0.1 broadcast_multiply_fusion
  9.7 0.1 fusion.37
  9.9 0.7 iota_compare_fusion.1
  10.6 6.6 %all-to-all-done = bf16[16,4,1152]{2,1,0:T(4,128)(2,1)S(1)} async-done(((bf16[16,4,1152]{2,1,0:T(4,128)(2,1)}), bf16[16,4,1152]{2,1,0:T(4,128)(2,1)S(1)}, u32[]{:S(2)}, u32[]{:S(2)}) %all-to-all-start) | async-done | bytes 147488 | tf_op jit(solution)/shard_map/all_to_all | solution.py:58
  17.3 0.1 slice_negate_fusion.1
  17.4 0.1 slice_negate_fusion
  17.5 0.2 convolution_convert_fusion.3
  17.8 0.5 convolution_convert_fusion.2
  18.2 3.5 %fusion.73 = (f32[4,8,16]{2,1,0:T(8,128)S(1)}, f32[4,8,16,512]{3,2,1,0:T(8,128)S(1)}) fusion(bf16[4,8,16,128]{3,2,1,0:T(8,128)(2,1)S(1)} %bitcast.63, pred[4,512]{1,0:T(4,128)(4,1)S(1)} %get-tuple-element.14, bf16[4,8,128]{2,1,0:T(8,128)(2,1)S(1)} %convolution_convert_fusion.3, pred[4,512]{1,0:T(4,128)(4,1)S(1)} %get-tuple-element.13, ...), kind=kOutput, calls=%fused_computation.95 | convolution fusion | flops 70255104 | bytes 5388288 | tf_op jit(solution)/shard_map/sub | solution.py:88
  21.8 2.9 %fusion.14 = bf16[4,8,16,128]{3,2,1,0:T(8,128)(2,1)S(1)} fusion(pred[4,512]{1,0:T(4,128)(4,1)S(1)} %get-tuple-element.14, bf16[4,8,128]{2,1,0:T(8,128)(2,1)S(1)} %get-tuple-element.10, f32[4,8,16,512]{3,2,1,0:T(8,128)S(1)} %get-tuple-element.16, f32[4,8,16]{2,1,0:T(8,128)S(1)} %get-tuple-element.15, bf16[4,512,1024]{2,1,0:T(8,128)(2,1)} %param.11), kind=kOutput, calls=%fused_computation.20 | convolution fusion | flops 69795840 | bytes 5386240 | tf_op jit(solution)/shard_map/rkgp,rpkd->rkgd/dot_general | solution.py:90
  24.7 0.4 fusion.15
  25.0 0.1 copy.64
  25.2 0.1 reshape.133
  25.2 0.1 copy.65
  25.4 9.7 %all_to_all.28 = bf16[1,1,4,8,2048]{4,2,1,0,3:T(4,128)(2,1)S(1)} all-to-all(bf16[1,1,4,8,2048]{4,2,1,0,3:T(4,128)(2,1)S(1)} %copy.65), channel_id=1, replica_groups=mesh['groups'=2,'gx'=8,'gy'=2] {'gx'}, dimensions={3} | all-to-all | bytes 262144 | tf_op jit(solution)/shard_map/all_to_all | solution.py:96
  35.1 0.1 copy.66
  35.2 2.0 %all-gather = bf16[8,2,1,4,1,2048]{5,0,4,3,2,1:T(8,128)(2,1)S(1)} all-gather(bf16[8,1,1,4,1,2048]{5,0,4,3,2,1:T(8,128)(2,1)S(1)} %copy.66), channel_id=2, replica_groups=mesh['groups'=2,'gx'=8,'gy'=2] {'gy'}, dimensions={1}, use_global_device_ids=true | all-gather | bytes 393216 | tf_op jit(solution)/shard_map/all_gather | solution.py:103
  37.2 0.2 copy.67
  37.4 0.1 reshape.134
  37.4 0.0 copy-start
  37.5 13.7 %fusion.1 = bf16[8,8,8192]{2,1,0:T(8,128)(2,1)S(1)} fusion(bf16[64,2048]{1,0:T(8,128)(2,1)S(1)} %reshape.134, bf16[2048,8192]{1,0:T(8,128)(2,1)} %param.13), kind=kOutput, calls=%fused_computation.2 | convolution fusion | flops 2148007936 | bytes 34865152 | tf_op jit(solution)/shard_map/dot_general | solution.py:105
  51.2 28.7 %all_to_all.29 = bf16[8,8,8192]{2,1,0:T(8,128)(2,1)S(1)} all-to-all(bf16[8,8,8192]{2,1,0:T(8,128)(2,1)S(1)} %fusion.1), channel_id=1, replica_groups=mesh['groups'=2,'gx'=8,'gy'=2] {'gx'}, dimensions={0} | all-to-all | bytes 2097152 | tf_op jit(solution)/shard_map/all_to_all | solution.py:107
  79.9 0.1 convert_reduce_fusion
  80.1 0.0 copy-done
  80.1 0.7 add_convert_fusion
  (6 shorter events, 0.1 us)
Async XLA Ops:
  1.6 15.6 %all-to-all-start = ((bf16[16,4,1152]{2,1,0:T(4,128)(2,1)}), bf16[16,4,1152]{2,1,0:T(4,128)(2,1)S(1)}, u32[]{:S(2)}, u32[]{:S(2)}) async-start(bf16[16,4,1152]{2,1,0:T(4,128)(2,1)} %reshape.128), calls=%async_computation | async-start | bytes 294912 | tf_op jit(solution)/shard_map/all_to_all | solution.py:58
  37.4 42.6 %copy-start = (bf16[8,8192]{1,0:T(8,128)(2,1)S(1)}, bf16[8,8192]{1,0:T(8,128)(2,1)}, u32[]{:S(2)}) copy-start(bf16[8,8192]{1,0:T(8,128)(2,1)} %param.7) | copy-start | bytes 393220

commit v2 on v1

v2 whole, which is shorter than its diff:
```python
import functools
import math

import jax
import jax.numpy as jnp
import numpy as np
from jax import lax
from jax.experimental import pallas as pl
from jax.experimental.pallas import tpu as pltpu
from jax.sharding import PartitionSpec as P

HEADS = 128
KV_HEADS = 8
HD = 128
GROUP = HEADS // KV_HEADS
ROPE_BASE = 500000.0
NORM = 1.0 / math.sqrt(HD)
MIX_NORM = 1.0 / math.sqrt(HEADS)
CHUNKS = (0.5, 0.5)
NEAR = 4
TILE = 512


def sign_table(order):
    bits = lax.broadcasted_iota(jnp.int32, (order, order), 0) & lax.broadcasted_iota(jnp.int32, (order, order), 1)
    step = 1
    while step < order.bit_length():
        step *= 2
    while step > 1:
        step //= 2
        bits = bits ^ (bits >> step)
    return (1 - 2 * (bits & 1)).astype(jnp.float32).astype(jnp.bfloat16)


def hadamard(rows, table):
    high = rows.astype(jnp.bfloat16)
    rest = rows - high.astype(jnp.float32)
    middle = rest.astype(jnp.bfloat16)
    low = (rest - middle.astype(jnp.float32)).astype(jnp.bfloat16)
    dot = functools.partial(jnp.dot, preferred_element_type=jnp.float32)
    return (dot(high, table) + (dot(middle, table) + dot(low, table))) * NORM


def put_row(buf, r, length, rows):
    base = pl.multiple_of((length >> 4) << 4, 16)
    here = lax.broadcasted_iota(jnp.int32, (16, HD), 0) == length - base
    for k in range(KV_HEADS):
        lanes = slice(k * HD, (k + 1) * HD)
        old = buf[r, pl.ds(base, 16), lanes].astype(jnp.float32)
        buf[r, pl.ds(base, 16), lanes] = jnp.where(here, rows[k:k + 1], old).astype(jnp.bfloat16)


def attend(
    lengths_ref, query_ref, keyval_ref, turn_ref, key_hbm, value_hbm,
    out_ref, key_buf, value_buf, key_sem, value_sem,
):
    row_count, slots = key_buf.shape[:2]
    copies = []
    for r in range(row_count):
        pair = (
            pltpu.make_async_copy(key_hbm.at[r], key_buf.at[r], key_sem.at[r]),
            pltpu.make_async_copy(value_hbm.at[r], value_buf.at[r], value_sem.at[r]),
        )
        for copy in pair:
            copy.start()
        copies.append(pair)
    table = sign_table(HD)
    turned = []
    for r in range(row_count):
        cos, sin = turn_ref[r, 0:1, :], turn_ref[r, 1:2, :]
        for vector in (query_ref[r].astype(jnp.float32), keyval_ref[r].astype(jnp.float32)):
            turned.append(vector * cos + pltpu.roll(vector, HD // 2, axis=1) * sin)
    turned = hadamard(jnp.concatenate(turned, axis=0), table)
    stride = HEADS + 2 * KV_HEADS
    head_of = lax.broadcasted_iota(jnp.int32, (HD, HEADS), 1) // GROUP
    slot = lax.broadcasted_iota(jnp.int32, (slots, HEADS), 0)
    for r in range(row_count):
        length = lengths_ref[r]
        across = jnp.transpose(turned[r * stride:r * stride + HEADS])
        spread = jnp.concatenate(
            [jnp.where(head_of == k, across, 0.0).astype(jnp.bfloat16) for k in range(KV_HEADS)], axis=0
        )
        copies[r][0].wait()
        new_key = turned[r * stride + HEADS:r * stride + HEADS + KV_HEADS]
        put_row(key_buf, r, length, new_key)
        scores = jnp.dot(key_buf[r], spread, preferred_element_type=jnp.float32) * NORM
        scores = jnp.where(slot <= length, scores, -jnp.inf)
        weights = jnp.exp(scores - jnp.max(scores, axis=0, keepdims=True))
        weights = weights * (1.0 / jnp.sum(weights, axis=0, keepdims=True))
        weights = jnp.transpose(weights).astype(jnp.bfloat16)
        copies[r][1].wait()
        put_row(value_buf, r, length, keyval_ref[r, KV_HEADS:].astype(jnp.float32))
        attended = []
        for k in range(0, KV_HEADS, 2):
            two = jnp.dot(
                weights[k * GROUP:(k + 2) * GROUP], value_buf[r, :, k * HD:(k + 2) * HD],
                preferred_element_type=jnp.float32,
            )
            attended += [two[:GROUP, :HD], two[GROUP:, HD:]]
        attended = jnp.concatenate(attended, axis=0).astype(jnp.bfloat16)
        mixed = jnp.dot(table, attended, preferred_element_type=jnp.float32) * MIX_NORM
        out_ref[:, r] = mixed.reshape(out_ref.shape[0], *out_ref.shape[2:]).astype(jnp.bfloat16)


def attention(lengths, query, keyval, turn, key_cache, value_cache, blocks):
    row_count, slots, width = key_cache.shape
    vmem, hbm = pl.BlockSpec(memory_space=pltpu.VMEM), pl.BlockSpec(memory_space=pltpu.HBM)
    key_cache = pltpu.with_memory_space_constraint(key_cache, pltpu.HBM)
    value_cache = pltpu.with_memory_space_constraint(value_cache, pltpu.HBM)
    return pl.pallas_call(
        attend,
        out_shape=jax.ShapeDtypeStruct((blocks, row_count, HEADS // blocks, HD), jnp.bfloat16),
        in_specs=[pl.BlockSpec(memory_space=pltpu.SMEM)] + [vmem] * 3 + [hbm] * 2,
        out_specs=vmem,
        scratch_shapes=[
            pltpu.VMEM((row_count, slots, width), jnp.bfloat16),
            pltpu.VMEM((row_count, slots, width), jnp.bfloat16),
            pltpu.SemaphoreType.DMA((row_count,)),
            pltpu.SemaphoreType.DMA((row_count,)),
        ],
        compiler_params=pltpu.CompilerParams(vmem_limit_bytes=32 * 2**20),
        cost_estimate=pl.CostEstimate(
            flops=4 * row_count * HEADS * slots * HD,
            bytes_accessed=4 * row_count * slots * width,
            transcendentals=row_count * HEADS * slots,
        ),
        name="attend",
    )(lengths, query, keyval, turn, key_cache, value_cache)


def project(first, place_ref, rows_ref, weight_hbm, own_ref, *rest):
    send_refs, (product_ref, weight_buf, weight_sem) = rest[:-3], rest[-3:]
    blocks = product_ref.shape[0]
    tiles = weight_buf.shape[0]
    copies = []
    for j in range(tiles):
        columns = pl.ds((first + j) * TILE, TILE)
        copies.append(pltpu.make_async_copy(weight_hbm.at[:, columns], weight_buf.at[j], weight_sem.at[j]))
        copies[-1].start()
    place = place_ref[0]
    for j in range(tiles):
        columns = slice(j * TILE, (j + 1) * TILE)
        copies[j].wait()
        product = jnp.dot(rows_ref[...], weight_buf[j], preferred_element_type=jnp.float32)
        product_ref[:, :, columns] = product.reshape(blocks, -1, TILE)
        for step in range(NEAR):
            taken = jnp.concatenate(
                [product_ref[NEAR * far + (place ^ step), :, columns] for far in range(blocks // NEAR)], axis=0
            )
            if step:
                send_refs[step - 1][:, columns] = taken.astype(jnp.bfloat16)
            else:
                own_ref[:, columns] = taken


def projection(place, rows, weight, first, count, blocks):
    row_count, depth = rows.shape
    out_rows = row_count // NEAR
    vmem = pl.BlockSpec(memory_space=pltpu.VMEM)
    shapes = [jax.ShapeDtypeStruct((out_rows, count * TILE), jnp.float32)]
    shapes += [jax.ShapeDtypeStruct((out_rows, count * TILE), jnp.bfloat16)] * (NEAR - 1)
    return pl.pallas_call(
        functools.partial(project, first),
        out_shape=shapes,
        in_specs=[pl.BlockSpec(memory_space=pltpu.SMEM), vmem, pl.BlockSpec(memory_space=pltpu.HBM)],
        out_specs=[vmem] * NEAR,
        scratch_shapes=[
            pltpu.VMEM((blocks, row_count // blocks, count * TILE), jnp.float32),
            pltpu.VMEM((count, depth, TILE), jnp.bfloat16),
            pltpu.SemaphoreType.DMA((count,)),
        ],
        compiler_params=pltpu.CompilerParams(vmem_limit_bytes=40 * 2**20),
        cost_estimate=pl.CostEstimate(
            flops=2 * row_count * depth * count * TILE,
            bytes_accessed=2 * depth * count * TILE,
            transcendentals=0,
        ),
        name="project",
    )(place, rows, pltpu.with_memory_space_constraint(weight, pltpu.HBM))


def shards(residual, query, new_keyval, key_cache, value_cache, lengths, out_weight):
    gx_count = lax.axis_size("gx")
    gx_index = lax.axis_index("gx")
    row_count = lengths.shape[0]
    query_width = query.shape[1]

    both = jnp.concatenate([query, new_keyval], axis=1).reshape(-1, row_count, query_width + new_keyval.shape[1])
    both = lax.all_to_all(both, ("gx", "gy"), split_axis=0, concat_axis=0, tiled=True)
    both = both.transpose(1, 0, 2)
    query_rows = both[:, :, :query_width].reshape(row_count, HEADS, HD)
    keyval_rows = both[:, :, query_width:].reshape(row_count, 2 * KV_HEADS, HD)

    frequency = ROPE_BASE ** (-2.0 * np.arange(HD // 2) / HD)
    frequency = np.concatenate([frequency, frequency]).astype(np.float32)
    side = np.where(np.arange(HD) < HD // 2, -1.0, 1.0).astype(np.float32)
    angles = lengths.astype(jnp.float32)[:, None] * frequency[None, :]
    turn = jnp.stack([jnp.cos(angles), jnp.sin(angles) * side], axis=1)

    bounded = jnp.minimum(lengths, key_cache.shape[1] - 1)
    mixed = attention(bounded, query_rows, keyval_rows, turn, key_cache, value_cache, gx_count)
    mixed = lax.all_to_all(mixed, "gx", split_axis=0, concat_axis=0, tiled=True)
    mixed = lax.all_gather(mixed, "gy", axis=1)
    feature_rows = mixed.reshape(gx_count * 2 * row_count, -1)

    near_place = jnp.reshape(gx_index % NEAR, (1,)).astype(jnp.int32)
    far_count = gx_count // NEAR
    far_place = gx_index // NEAR
    block_rows = feature_rows.shape[0] // gx_count
    tiles = out_weight.shape[1] // TILE
    outs = []
    first = 0
    for share in CHUNKS:
        count = int(round(tiles * share))
        columns = slice(first * TILE, (first + count) * TILE)
        own, *sends = projection(near_place, feature_rows, out_weight, first, count, gx_count)
        total = own
        for step, send in enumerate(sends, 1):
            got = lax.ppermute(send, "gx", [(i, i ^ step) for i in range(gx_count)])
            total = total + got.astype(jnp.float32)
        total = total.reshape(far_count, block_rows, count * TILE)
        if far_count == 2:
            low, high = total[0], total[1]
            mine = jnp.where(far_place == 0, low, high)
            send = jnp.where(far_place == 0, high, low).astype(jnp.bfloat16)
            got = lax.ppermute(send, "gx", [(i, i ^ NEAR) for i in range(gx_count)])
            summed = mine + got.astype(jnp.float32)
        elif far_count > 1:
            parts = [[near + NEAR * far for far in range(far_count)] for near in range(NEAR)]
            got = lax.all_to_all(
                total.astype(jnp.bfloat16), "gx", split_axis=0, concat_axis=0,
                axis_index_groups=parts, tiled=True,
            )
            summed = jnp.sum(got.astype(jnp.float32), axis=0)
        else:
            summed = total[0]
        outs.append((residual[:, columns].astype(jnp.float32) + summed).astype(jnp.bfloat16))
        first += count
    return jnp.concatenate(outs, axis=1)


def solution(mesh):
    in_specs = (
        P(("groups", "gx"), "gy"),
        P("groups", ("gx", "gy")),
        P("groups", ("gx", "gy")),
        P(("groups", "gx", "gy"), None, None),
        P(("groups", "gx", "gy"), None, None),
        P(("groups", "gx", "gy")),
        P("gx", "gy"),
    )
    out_specs = P(("groups", "gx"), "gy")
    return jax.shard_map(shards, mesh=mesh, in_specs=in_specs, out_specs=out_specs, check_vma=False)
```

time: 81.2 us -> 72.2 us (0.89)
  blocking collectives: 40.5 us -> 1.98 us
  Pallas kernels: 0 us -> 21.8 us
  matrix products: 21.2 us -> 0 us
  waiting for transfers between devices: 6.6 us -> 25.1 us
  starting transfers between devices: 7.36 us -> 18.4 us
    all_to_all x2 -> x0, blocking collectives: 38.5 us -> none  [the longest x1 28.7 us: shards(): lax.all_to_all(partial, 'gx', split_axis=0, concat_axis=0, tiled=True)]
    pallas_call x0 -> x3, Pallas kernels: none -> 21.8 us  [the longest x2 13.1 us: projection(): pl.pallas_call(functools.partial(project, first), out_shape=shapes, in_sp...]
    dot_general x5 -> x0, matrix products: 17.7 us -> none  [the longest x1 13.7 us: shards(): jnp.dot(feature_rows, out_weight, preferred_element_type=jnp.float32)]
    ppermute x0 -> x8, waiting for transfers between devices: none -> 11.2 us  [the longest x6 6.08 us: shards(): got = lax.ppermute(send, 'gx', [(i, i ^ step) for i in range(gx_count)])]
    ppermute x0 -> x8, starting transfers between devices: none -> 7.63 us  [the longest x6 7.11 us: shards(): got = lax.ppermute(send, 'gx', [(i, i ^ step) for i in range(gx_count)])]
    all_to_all x1 -> x2, waiting for transfers between devices: 6.6 us -> 13.9 us  [the longest x1 7.27 us: shards(): mixed = lax.all_to_all(mixed, 'gx', split_axis=0, concat_axis=0, tiled=True)]
    sub x1 -> x0, matrix products: 3.52 us -> none  [shards(): weights = jnp.exp(scores - row_max)]
    all_to_all x1 -> x2, starting transfers between devices: 7.36 us -> 10.7 us  [the longest x1 7.36 us: shards(): lax.all_to_all(both, ('gx', 'gy'), split_axis=0, concat_axis=0, tiled=True)]
  transfers between devices with their start and end apart: 1 -> 10, of which waited for: 1 -> 6; matrix products, arithmetic and copies ran while one was open for 2% -> 2% of each run, Pallas kernels for 0% -> 9%
where the time goes in v2:
time: 72.2 us; the launch traced here: 71.7 us
  waiting for transfers between devices  25.1 us (35%)
  Pallas kernels  21.8 us (30%)
  starting transfers between devices  18.4 us (25%)
  other arithmetic  3.29 us (5%)
  blocking collectives  1.98 us (3%)
  local copies, waits for them, and re-layouts  0.95 us (1%)
    pallas_call x2, Pallas kernels, projection(): pl.pallas_call(functools.partial(project, first), out_shape=shapes, in_sp...  13.1 us
    pallas_call x1, Pallas kernels, attention(): pl.pallas_call(attend, out_shape=jax.ShapeDtypeStruct((blocks, row_count,...  8.76 us
    all_to_all x1, starting transfers between devices, shards(): lax.all_to_all(both, ('gx', 'gy'), split_axis=0, concat_axis=0, tiled=True)  7.36 us
    all_to_all x1, waiting for transfers between devices, shards(): mixed = lax.all_to_all(mixed, 'gx', split_axis=0, concat_axis=0, tiled=True)  7.27 us
    ppermute x6, starting transfers between devices, shards(): got = lax.ppermute(send, 'gx', [(i, i ^ step) for i in range(gx_count)])  7.11 us
    all_to_all x1, waiting for transfers between devices, shards(): lax.all_to_all(both, ('gx', 'gy'), split_axis=0, concat_axis=0, tiled=True)  6.63 us
    ppermute x6, waiting for transfers between devices, shards(): got = lax.ppermute(send, 'gx', [(i, i ^ step) for i in range(gx_count)])  6.08 us
    ppermute x2, waiting for transfers between devices, shards(): got = lax.ppermute(send, 'gx', [(i, i ^ NEAR) for i in range(gx_count)])  5.14 us
  transfers between devices with their start and end apart: 10, of which 6 were waited for; matrix products, arithmetic and copies ran while one was open for 2% of the time, Pallas kernels for 9%

profile of v2, /device:TPU:0, one launch (start us, length us, event | category | flops | bytes accessed | tf_op | source)
XLA Modules:
  0.0 71.7 jit_solution(1980395221604598672)
XLA Ops:
  0.0 0.9 %pad_maximum_fusion = bf16[64,1152]{1,0:T(8,128)(2,1)S(1)} fusion(bf16[64,128]{1,0:T(8,128)(2,1)} %param.11, bf16[64,1024]{1,0:T(8,128)(2,1)} %param.10), kind=kLoop, calls=%fused_computation.3 | loop fusion | flops 294912 | bytes 294912 | tf_op jit(solution)/shard_map/concatenate | solution.py:188
  0.9 0.7 reshape.135
  1.6 7.4 %all-to-all-start = ((bf16[16,4,1152]{2,1,0:T(4,128)(2,1)}), bf16[16,4,1152]{2,1,0:T(4,128)(2,1)S(1)}, u32[]{:S(2)}, u32[]{:S(2)}) async-start(bf16[16,4,1152]{2,1,0:T(4,128)(2,1)} %reshape.135), calls=%async_computation | async-start | bytes 294912 | tf_op jit(solution)/shard_map/all_to_all | solution.py:189
  9.0 0.7 %fusion = (f32[4]{0:T(128)S(1)}, s32[4]{0:T(128)S(1)}) fusion(s32[4]{0:T(128)} %param.14), kind=kLoop, calls=%fused_computation.14 | loop fusion | flops 8 | bytes 48 | tf_op jit(solution)/shard_map/convert_element_type | solution.py:197
  9.8 0.1 mul.39
  9.8 0.7 %multiply_cosine_fusion = (f32[4,1,128]{2,1,0:T(1,128)S(1)}, f32[4,1,128]{2,1,0:T(1,128)S(1)}) fusion(f32[4,1,128]{2,1,0:T(1,128)S(1)} %bitcast.14, f32[128]{0:T(128)} %constant.45, f32[128]{0:T(128)} %constant.40.clone), kind=kLoop, calls=%fused_computation.12 | loop fusion | flops 1024 | bytes 7168 | tf_op jit(solution)/shard_map/cos | solution.py:198
  10.6 6.6 %all-to-all-done = bf16[16,4,1152]{2,1,0:T(4,128)(2,1)S(1)} async-done(((bf16[16,4,1152]{2,1,0:T(4,128)(2,1)}), bf16[16,4,1152]{2,1,0:T(4,128)(2,1)S(1)}, u32[]{:S(2)}, u32[]{:S(2)}) %all-to-all-start) | async-done | bytes 147488 | tf_op jit(solution)/shard_map/all_to_all | solution.py:189
  17.3 0.1 reshape.136.query_ref
  17.3 8.8 %attend.1 = bf16[8,4,16,128]{3,2,1,0:T(8,128)(2,1)} custom-call(s32[4]{0:T(128)S(1)} %get-tuple-element.26.lengths_ref, bf16[4,128,128]{2,1,0:T(8,128)(2,1)S(1)} %reshape.136.query_ref, bf16[4,16,128]{2,1,0:T(8,128)(2,1)S(1)} %slice.37.keyval_ref, f32[4,2,128]{2,1,0:T(2,128)S(1)} %pad_maximum_fusion.2.turn_ref, bf16[4,512,1024]{2,1,0:T(8,128)(2,1)} %key_hbm.1, ...), custom_call_target="tpu_custom_call" | custom-call | flops 134217728 | bytes 8388608 | tf_op jit(solution)/shard_map/attend/pallas_call | solution.py:110
  26.1 3.4 %all-to-all-start.1 = ((bf16[8,4,16,128]{3,2,1,0:T(8,128)(2,1)}), bf16[8,4,16,128]{3,2,1,0:T(8,128)(2,1)S(1)}, u32[]{:S(2)}, u32[]{:S(2)}) async-start(bf16[8,4,16,128]{3,2,1,0:T(8,128)(2,1)} %attend.1), calls=%async_computation.1 | async-start | bytes 262144 | tf_op jit(solution)/shard_map/all_to_all | solution.py:202
  29.5 7.3 %all-to-all-done.1 = bf16[8,4,16,128]{3,2,1,0:T(8,128)(2,1)S(1)} async-done(((bf16[8,4,16,128]{3,2,1,0:T(8,128)(2,1)}), bf16[8,4,16,128]{3,2,1,0:T(8,128)(2,1)S(1)}, u32[]{:S(2)}, u32[]{:S(2)}) %all-to-all-start.1) | async-done | bytes 131104 | tf_op jit(solution)/shard_map/all_to_all | solution.py:202
  36.8 2.0 %all-gather = bf16[8,8,16,128]{3,2,1,0:T(8,128)(2,1)S(1)} all-gather(bf16[8,4,16,128]{3,2,1,0:T(8,128)(2,1)S(1)} %all-to-all-done.1), channel_id=2, replica_groups=mesh['groups'=2,'gx'=8,'gy'=2] {'gy'}, dimensions={1}, use_global_device_ids=true | all-gather | bytes 393216 | tf_op jit(solution)/shard_map/all_gather | solution.py:203
  38.8 0.1 copy.17
  38.8 6.5 %project.3 = (f32[16,4096]{1,0:T(8,128)S(1)}, bf16[16,4096]{1,0:T(8,128)(2,1)S(1)}, bf16[16,4096]{1,0:T(8,128)(2,1)S(1)}, bf16[16,4096]{1,0:T(8,128)(2,1)S(1)}) custom-call(s32[1]{0:T(128)} %bitcast.place_ref, bf16[64,2048]{1,0:T(8,128)(2,1)S(1)} %bitcast.10, bf16[2048,8192]{1,0:T(8,128)(2,1)} %weight_hbm.3), custom_call_target="tpu_custom_call" | custom-call | flops 1073741824 | bytes 16777216 | tf_op jit(solution)/shard_map/project/pallas_call | solution.py:162
  45.4 0.3 collective-permute-start.4
  45.6 1.1 %collective-permute-start.5 = (bf16[16,4096]{1,0:T(8,128)(2,1)S(1)}, bf16[16,4096]{1,0:T(8,128)(2,1)S(1)}, u32[]{:S(2)}, u32[]{:S(2)}) collective-permute-start(bf16[16,4096]{1,0:T(8,128)(2,1)S(1)} %get-tuple-element.19), channel_id=1, source_target_pairs={{0,4},{2,6},{4,0},{6,2},{8,12},{10,14},{12,8},{14,10},{1,5},{3,7},... | collective-permute-start | bytes 393224 | tf_op jit(solution)/shard_map/ppermute | solution.py:219
  46.7 2.2 %collective-permute-start.6 = (bf16[16,4096]{1,0:T(8,128)(2,1)S(1)}, bf16[16,4096]{1,0:T(8,128)(2,1)S(1)}, u32[]{:S(2)}, u32[]{:S(2)}) collective-permute-start(bf16[16,4096]{1,0:T(8,128)(2,1)S(1)} %get-tuple-element.20), channel_id=1, source_target_pairs={{0,6},{2,4},{4,2},{6,0},{8,14},{10,12},{12,10},{14,8},{1,7},{3,5},... | collective-permute-start | bytes 393224 | tf_op jit(solution)/shard_map/ppermute | solution.py:219
  48.9 0.0 copy-start
  48.9 6.6 %project.2 = (f32[16,4096]{1,0:T(8,128)S(1)}, bf16[16,4096]{1,0:T(8,128)(2,1)S(1)}, bf16[16,4096]{1,0:T(8,128)(2,1)S(1)}, bf16[16,4096]{1,0:T(8,128)(2,1)S(1)}) custom-call(s32[1]{0:T(128)} %bitcast.place_ref, bf16[64,2048]{1,0:T(8,128)(2,1)S(1)} %bitcast.11, bf16[2048,8192]{1,0:T(8,128)(2,1)} %weight_hbm.3), custom_call_target="tpu_custom_call" | custom-call | flops 1073741824 | bytes 16777216 | tf_op jit(solution)/shard_map/project/pallas_call | solution.py:162
  55.5 0.3 collective-permute-start
  55.8 1.1 %collective-permute-start.1 = (bf16[16,4096]{1,0:T(8,128)(2,1)S(1)}, bf16[16,4096]{1,0:T(8,128)(2,1)S(1)}, u32[]{:S(2)}, u32[]{:S(2)}) collective-permute-start(bf16[16,4096]{1,0:T(8,128)(2,1)S(1)} %get-tuple-element.15), channel_id=1, source_target_pairs={{0,4},{2,6},{4,0},{6,2},{8,12},{10,14},{12,8},{14,10},{1,5},{3,7},... | collective-permute-start | bytes 393224 | tf_op jit(solution)/shard_map/ppermute | solution.py:219
  56.9 0.0 collective-permute-done.4
  56.9 2.2 %collective-permute-start.2 = (bf16[16,4096]{1,0:T(8,128)(2,1)S(1)}, bf16[16,4096]{1,0:T(8,128)(2,1)S(1)}, u32[]{:S(2)}, u32[]{:S(2)}) collective-permute-start(bf16[16,4096]{1,0:T(8,128)(2,1)S(1)} %get-tuple-element.16), channel_id=1, source_target_pairs={{0,6},{2,4},{4,2},{6,0},{8,14},{10,12},{12,10},{14,8},{1,7},{3,5},... | collective-permute-start | bytes 393224 | tf_op jit(solution)/shard_map/ppermute | solution.py:219
  59.0 0.0 collective-permute-done.5
  59.0 0.0 collective-permute-done.6
  59.0 0.1 convert_add_fusion
  59.1 0.5 collective-permute-start.7
  59.6 1.7 %collective-permute-done = bf16[16,4096]{1,0:T(8,128)(2,1)S(1)} collective-permute-done((bf16[16,4096]{1,0:T(8,128)(2,1)S(1)}, bf16[16,4096]{1,0:T(8,128)(2,1)S(1)}, u32[]{:S(2)}, u32[]{:S(2)}) %collective-permute-start) | collective-permute-done | bytes 131104 | tf_op jit(solution)/shard_map/ppermute | solution.py:219
  61.3 1.1 %collective-permute-done.1 = bf16[16,4096]{1,0:T(8,128)(2,1)S(1)} collective-permute-done((bf16[16,4096]{1,0:T(8,128)(2,1)S(1)}, bf16[16,4096]{1,0:T(8,128)(2,1)S(1)}, u32[]{:S(2)}, u32[]{:S(2)}) %collective-permute-start.1) | collective-permute-done | bytes 131104 | tf_op jit(solution)/shard_map/ppermute | solution.py:219
  62.4 3.2 %collective-permute-done.2 = bf16[16,4096]{1,0:T(8,128)(2,1)S(1)} collective-permute-done((bf16[16,4096]{1,0:T(8,128)(2,1)S(1)}, bf16[16,4096]{1,0:T(8,128)(2,1)S(1)}, u32[]{:S(2)}, u32[]{:S(2)}) %collective-permute-start.2) | collective-permute-done | bytes 131104 | tf_op jit(solution)/shard_map/ppermute | solution.py:219
  65.7 0.1 convert_add_fusion.1
  65.7 0.1 collective-permute-start.3
  65.8 0.0 collective-permute-done.7
  65.8 5.1 %collective-permute-done.3 = bf16[8,4096]{1,0:T(8,128)(2,1)S(1)} collective-permute-done((bf16[8,4096]{1,0:T(8,128)(2,1)S(1)}, bf16[8,4096]{1,0:T(8,128)(2,1)S(1)}, u32[]{:S(2)}, u32[]{:S(2)}) %collective-permute-start.3) | collective-permute-done | bytes 65568 | tf_op jit(solution)/shard_map/ppermute | solution.py:226
  71.0 0.0 copy-done
  71.0 0.1 add_convert_fusion.1
  71.0 0.7 pad_maximum_fusion.1
  (6 shorter events, 0.1 us)
Async XLA Ops:
  1.6 15.6 %all-to-all-start = ((bf16[16,4,1152]{2,1,0:T(4,128)(2,1)}), bf16[16,4,1152]{2,1,0:T(4,128)(2,1)S(1)}, u32[]{:S(2)}, u32[]{:S(2)}) async-start(bf16[16,4,1152]{2,1,0:T(4,128)(2,1)} %reshape.135), calls=%async_computation | async-start | bytes 294912 | tf_op jit(solution)/shard_map/all_to_all | solution.py:189
  26.1 10.7 %all-to-all-start.1 = ((bf16[8,4,16,128]{3,2,1,0:T(8,128)(2,1)}), bf16[8,4,16,128]{3,2,1,0:T(8,128)(2,1)S(1)}, u32[]{:S(2)}, u32[]{:S(2)}) async-start(bf16[8,4,16,128]{3,2,1,0:T(8,128)(2,1)} %attend.1), calls=%async_computation.1 | async-start | bytes 262144 | tf_op jit(solution)/shard_map/all_to_all | solution.py:202
  45.4 11.5 %collective-permute-start.4 = (bf16[16,4096]{1,0:T(8,128)(2,1)S(1)}, bf16[16,4096]{1,0:T(8,128)(2,1)S(1)}, u32[]{:S(2)}, u32[]{:S(2)}) collective-permute-start(bf16[16,4096]{1,0:T(8,128)(2,1)S(1)} %get-tuple-element.18), channel_id=1, source_target_pairs={{0,2},{2,0},{4,6},{6,4},{8,10},{10,8},{12,14},{14,12},{1,3},{3,1},... | collective-permute-start | bytes 393224 | tf_op jit(solution)/shard_map/ppermute | solution.py:219
  45.6 13.4 %collective-permute-start.5 = (bf16[16,4096]{1,0:T(8,128)(2,1)S(1)}, bf16[16,4096]{1,0:T(8,128)(2,1)S(1)}, u32[]{:S(2)}, u32[]{:S(2)}) collective-permute-start(bf16[16,4096]{1,0:T(8,128)(2,1)S(1)} %get-tuple-element.19), channel_id=1, source_target_pairs={{0,4},{2,6},{4,0},{6,2},{8,12},{10,14},{12,8},{14,10},{1,5},{3,7},... | collective-permute-start | bytes 393224 | tf_op jit(solution)/shard_map/ppermute | solution.py:219
  46.7 12.3 %collective-permute-start.6 = (bf16[16,4096]{1,0:T(8,128)(2,1)S(1)}, bf16[16,4096]{1,0:T(8,128)(2,1)S(1)}, u32[]{:S(2)}, u32[]{:S(2)}) collective-permute-start(bf16[16,4096]{1,0:T(8,128)(2,1)S(1)} %get-tuple-element.20), channel_id=1, source_target_pairs={{0,6},{2,4},{4,2},{6,0},{8,14},{10,12},{12,10},{14,8},{1,7},{3,5},... | collective-permute-start | bytes 393224 | tf_op jit(solution)/shard_map/ppermute | solution.py:219
  48.9 22.1 %copy-start = (bf16[8,8192]{1,0:T(8,128)(2,1)S(1)}, bf16[8,8192]{1,0:T(8,128)(2,1)}, u32[]{:S(2)}) copy-start(bf16[8,8192]{1,0:T(8,128)(2,1)} %param.9) | copy-start | bytes 393220
  55.5 5.8 %collective-permute-start = (bf16[16,4096]{1,0:T(8,128)(2,1)S(1)}, bf16[16,4096]{1,0:T(8,128)(2,1)S(1)}, u32[]{:S(2)}, u32[]{:S(2)}) collective-permute-start(bf16[16,4096]{1,0:T(8,128)(2,1)S(1)} %get-tuple-element.14), channel_id=1, source_target_pairs={{0,2},{2,0},{4,6},{6,4},{8,10},{10,8},{12,14},{14,12},{1,3},{3,1},... | collective-permute-start | bytes 393224 | tf_op jit(solution)/shard_map/ppermute | solution.py:219
  55.8 6.7 %collective-permute-start.1 = (bf16[16,4096]{1,0:T(8,128)(2,1)S(1)}, bf16[16,4096]{1,0:T(8,128)(2,1)S(1)}, u32[]{:S(2)}, u32[]{:S(2)}) collective-permute-start(bf16[16,4096]{1,0:T(8,128)(2,1)S(1)} %get-tuple-element.15), channel_id=1, source_target_pairs={{0,4},{2,6},{4,0},{6,2},{8,12},{10,14},{12,8},{14,10},{1,5},{3,7},... | collective-permute-start | bytes 393224 | tf_op jit(solution)/shard_map/ppermute | solution.py:219
  56.9 8.8 %collective-permute-start.2 = (bf16[16,4096]{1,0:T(8,128)(2,1)S(1)}, bf16[16,4096]{1,0:T(8,128)(2,1)S(1)}, u32[]{:S(2)}, u32[]{:S(2)}) collective-permute-start(bf16[16,4096]{1,0:T(8,128)(2,1)S(1)} %get-tuple-element.16), channel_id=1, source_target_pairs={{0,6},{2,4},{4,2},{6,0},{8,14},{10,12},{12,10},{14,8},{1,7},{3,5},... | collective-permute-start | bytes 393224 | tf_op jit(solution)/shard_map/ppermute | solution.py:219
  59.1 6.7 %collective-permute-start.7 = (bf16[8,4096]{1,0:T(8,128)(2,1)S(1)}, bf16[8,4096]{1,0:T(8,128)(2,1)S(1)}, u32[]{:S(2)}, u32[]{:S(2)}) collective-permute-start(bf16[8,4096]{1,0:T(8,128)(2,1)S(1)} %select_convert_fusion), channel_id=1, source_target_pairs={{0,8},{2,10},{4,12},{6,14},{8,0},{10,2},{12,4},{14,6},{1,9},{3,11}... | collective-permute-start | bytes 196616 | tf_op jit(solution)/shard_map/ppermute | solution.py:226
  65.7 5.2 %collective-permute-start.3 = (bf16[8,4096]{1,0:T(8,128)(2,1)S(1)}, bf16[8,4096]{1,0:T(8,128)(2,1)S(1)}, u32[]{:S(2)}, u32[]{:S(2)}) collective-permute-start(bf16[8,4096]{1,0:T(8,128)(2,1)S(1)} %select_convert_fusion.1), channel_id=1, source_target_pairs={{0,8},{2,10},{4,12},{6,14},{8,0},{10,2},{12,4},{14,6},{1,9},{3,11}... | collective-permute-start | bytes 196616 | tf_op jit(solution)/shard_map/ppermute | solution.py:226

commit v3 on v2

v3 whole, which is shorter than its diff:
```python
import functools
import math

import jax
import jax.numpy as jnp
import numpy as np
from jax import lax
from jax.experimental import pallas as pl
from jax.experimental.pallas import tpu as pltpu
from jax.sharding import PartitionSpec as P

HEADS = 128
KV_HEADS = 8
HD = 128
GROUP = HEADS // KV_HEADS
ROPE_BASE = 500000.0
NORM = 1.0 / math.sqrt(HD)
MIX_NORM = 1.0 / math.sqrt(HEADS)
CHUNKS = (0.375, 0.625)
NEAR = 4
TILE = 512
LEAD = 4


def sign_table(order):
    bits = lax.broadcasted_iota(jnp.int32, (order, order), 0) & lax.broadcasted_iota(jnp.int32, (order, order), 1)
    step = 1
    while step < order.bit_length():
        step *= 2
    while step > 1:
        step //= 2
        bits = bits ^ (bits >> step)
    return (1 - 2 * (bits & 1)).astype(jnp.float32).astype(jnp.bfloat16)


def hadamard(rows, table):
    high = rows.astype(jnp.bfloat16)
    rest = rows - high.astype(jnp.float32)
    middle = rest.astype(jnp.bfloat16)
    low = (rest - middle.astype(jnp.float32)).astype(jnp.bfloat16)
    dot = functools.partial(jnp.dot, preferred_element_type=jnp.float32)
    return (dot(high, table) + (dot(middle, table) + dot(low, table))) * NORM


def put_row(buf, length, rows):
    base = pl.multiple_of((length >> 4) << 4, 16)
    here = lax.broadcasted_iota(jnp.int32, (16, HD), 0) == length - base
    for k in range(KV_HEADS):
        lanes = slice(k * HD, (k + 1) * HD)
        old = buf[pl.ds(base, 16), lanes].astype(jnp.float32)
        buf[pl.ds(base, 16), lanes] = jnp.where(here, rows[k:k + 1], old).astype(jnp.bfloat16)


def attend(
    first, lengths_ref, query_ref, keyval_ref, turn_ref, key_hbm, value_hbm, weight_hbm,
    out_ref, lead_ref, *scratch,
):
    row_count = lengths_ref.shape[0]
    key_bufs, value_bufs = scratch[:row_count], scratch[row_count:2 * row_count]
    sem = scratch[-1]
    slots = key_bufs[0].shape[0]
    requests = range(row_count)
    key_copies = [pltpu.make_async_copy(key_hbm.at[r], key_bufs[r], sem.at[r]) for r in requests]
    value_copies = [pltpu.make_async_copy(value_hbm.at[r], value_bufs[r], sem.at[row_count + r]) for r in requests]
    lead_copies = [
        pltpu.make_async_copy(
            weight_hbm.at[:, pl.ds((first + j) * TILE, TILE)], lead_ref.at[j], sem.at[2 * row_count + j]
        )
        for j in range(lead_ref.shape[0])
    ]
    for copy in key_copies + value_copies + lead_copies:
        copy.start()
    table = sign_table(HD)
    turned = []
    for r in requests:
        cos, sin = turn_ref[r, 0:1, :], turn_ref[r, 1:2, :]
        for vector in (query_ref[r].astype(jnp.float32), keyval_ref[r].astype(jnp.float32)):
            turned.append(vector * cos + pltpu.roll(vector, HD // 2, axis=1) * sin)
    turned = hadamard(jnp.concatenate(turned, axis=0), table)
    stride = HEADS + 2 * KV_HEADS
    head_of = lax.broadcasted_iota(jnp.int32, (HD, HEADS), 1) // GROUP
    spread = []
    for r in requests:
        across = jnp.transpose(turned[r * stride:r * stride + HEADS])
        spread.append(jnp.concatenate(
            [jnp.where(head_of == k, across, 0.0).astype(jnp.bfloat16) for k in range(KV_HEADS)], axis=0
        ))
    for r in requests:
        key_copies[r].wait()
        put_row(key_bufs[r], lengths_ref[r], turned[r * stride + HEADS:r * stride + HEADS + KV_HEADS])
    slot = lax.broadcasted_iota(jnp.int32, (slots, HEADS), 0)
    weights = []
    for r in requests:
        scores = jnp.dot(key_bufs[r][...], spread[r], preferred_element_type=jnp.float32) * NORM
        scores = jnp.where(slot <= lengths_ref[r], scores, -jnp.inf)
        lifted = jnp.exp(scores - jnp.max(scores, axis=0, keepdims=True))
        lifted = lifted * (1.0 / jnp.sum(lifted, axis=0, keepdims=True))
        weights.append(jnp.transpose(lifted.astype(jnp.bfloat16)))
    for r in requests:
        value_copies[r].wait()
        put_row(value_bufs[r], lengths_ref[r], keyval_ref[r, KV_HEADS:].astype(jnp.float32))
    for r in requests:
        attended = []
        for k in range(0, KV_HEADS, 2):
            two = jnp.dot(
                weights[r][k * GROUP:(k + 2) * GROUP], value_bufs[r][:, k * HD:(k + 2) * HD],
                preferred_element_type=jnp.float32,
            )
            attended += [two[:GROUP, :HD], two[GROUP:, HD:]]
        attended = jnp.concatenate(attended, axis=0).astype(jnp.bfloat16)
        mixed = jnp.dot(table, attended, preferred_element_type=jnp.float32) * MIX_NORM
        out_ref[:, r] = mixed.reshape(out_ref.shape[0], *out_ref.shape[2:]).astype(jnp.bfloat16)
    for copy in lead_copies:
        copy.wait()


def attention(lengths, query, keyval, turn, key_cache, value_cache, weight, first, blocks):
    row_count, slots, width = key_cache.shape
    vmem, hbm = pl.BlockSpec(memory_space=pltpu.VMEM), pl.BlockSpec(memory_space=pltpu.HBM)
    key_cache = pltpu.with_memory_space_constraint(key_cache, pltpu.HBM)
    value_cache = pltpu.with_memory_space_constraint(value_cache, pltpu.HBM)
    weight = pltpu.with_memory_space_constraint(weight, pltpu.HBM)
    return pl.pallas_call(
        functools.partial(attend, first),
        out_shape=(
            jax.ShapeDtypeStruct((blocks, row_count, HEADS // blocks, HD), jnp.bfloat16),
            pltpu.VMEM((LEAD, weight.shape[0], TILE), jnp.bfloat16),
        ),
        in_specs=[pl.BlockSpec(memory_space=pltpu.SMEM)] + [vmem] * 3 + [hbm] * 3,
        out_specs=(vmem, vmem),
        scratch_shapes=[pltpu.VMEM((slots, width), jnp.bfloat16)] * (2 * row_count)
        + [pltpu.SemaphoreType.DMA((2 * row_count + LEAD,))],
        compiler_params=pltpu.CompilerParams(vmem_limit_bytes=32 * 2**20),
        cost_estimate=pl.CostEstimate(
            flops=4 * row_count * HEADS * slots * HD,
            bytes_accessed=4 * row_count * slots * width,
            transcendentals=row_count * HEADS * slots,
        ),
        name="attend",
    )(lengths, query, keyval, turn, key_cache, value_cache, weight)


def arrange(core_ref, mine_ref, other_ref, out_ref, wide_ref):
    sources, row_count, heads, _ = mine_ref.shape
    core = core_ref[0]
    shape = (sources, row_count * heads, HD)
    wide_ref[:, core] = mine_ref[...].astype(jnp.float32).reshape(shape)
    wide_ref[:, 1 - core] = other_ref[...].astype(jnp.float32).reshape(shape)
    flat = wide_ref.reshape(sources * 2 * row_count * heads, HD)
    for g in range(heads):
        rows = flat[pl.ds(g, sources * 2 * row_count, stride=heads), :]
        out_ref[:, g * HD:(g + 1) * HD] = rows.astype(jnp.bfloat16)


def arrangement(core, mine, other):
    sources, row_count, heads, width = mine.shape
    if heads % 16:
        both = jnp.stack(
            [jnp.where(core[0] == 0, mine, other), jnp.where(core[0] == 0, other, mine)], axis=1
        )
        return both.reshape(sources * 2 * row_count, heads * width)
    vmem = pl.BlockSpec(memory_space=pltpu.VMEM)
    return pl.pallas_call(
        arrange,
        out_shape=jax.ShapeDtypeStruct((sources * 2 * row_count, heads * width), jnp.bfloat16),
        in_specs=[pl.BlockSpec(memory_space=pltpu.SMEM), vmem, vmem],
        out_specs=vmem,
        scratch_shapes=[pltpu.VMEM((sources, 2, row_count * heads, width), jnp.float32)],
        compiler_params=pltpu.CompilerParams(vmem_limit_bytes=8 * 2**20),
        name="arrange",
    )(core, mine, other)


def project(first, lead, place_ref, rows_ref, weight_hbm, *rest):
    product_ref, weight_buf, weight_sem = rest[-3:]
    own_ref, *send_refs = rest[-3 - NEAR:-3]
    blocks = product_ref.shape[0]
    tiles = lead + weight_buf.shape[0]
    weights = [rest[0].at[j] for j in range(lead)] + [weight_buf.at[j] for j in range(tiles - lead)]
    copies = [None] * lead
    for j in range(lead, tiles):
        columns = pl.ds((first + j) * TILE, TILE)
        copies.append(pltpu.make_async_copy(weight_hbm.at[:, columns], weights[j], weight_sem.at[j - lead]))
        copies[-1].start()
    place = place_ref[0]
    for j in range(tiles):
        columns = slice(j * TILE, (j + 1) * TILE)
        if copies[j] is not None:
            copies[j].wait()
        product = jnp.dot(rows_ref[...], weights[j][...], preferred_element_type=jnp.float32)
        product_ref[:, :, columns] = product.reshape(blocks, -1, TILE)
        for step in range(NEAR):
            taken = jnp.concatenate(
                [product_ref[NEAR * far + (place ^ step), :, columns] for far in range(blocks // NEAR)], axis=0
            )
            if step:
                send_refs[step - 1][:, columns] = taken.astype(jnp.bfloat16)
            else:
                own_ref[:, columns] = taken


def projection(place, rows, weight, lead, first, count, blocks):
    row_count, depth = rows.shape
    out_rows = row_count // NEAR
    leads = len(lead) and lead[0].shape[0]
    vmem = pl.BlockSpec(memory_space=pltpu.VMEM)
    shapes = [jax.ShapeDtypeStruct((out_rows, count * TILE), jnp.float32)]
    shapes += [jax.ShapeDtypeStruct((out_rows, count * TILE), jnp.bfloat16)] * (NEAR - 1)
    return pl.pallas_call(
        functools.partial(project, first, leads),
        out_shape=shapes,
        in_specs=[pl.BlockSpec(memory_space=pltpu.SMEM), vmem, pl.BlockSpec(memory_space=pltpu.HBM)] + [vmem] * len(lead),
        out_specs=[vmem] * NEAR,
        scratch_shapes=[
            pltpu.VMEM((blocks, row_count // blocks, count * TILE), jnp.float32),
            pltpu.VMEM((count - leads, depth, TILE), jnp.bfloat16),
            pltpu.SemaphoreType.DMA((count - leads,)),
        ],
        compiler_params=pltpu.CompilerParams(vmem_limit_bytes=40 * 2**20),
        cost_estimate=pl.CostEstimate(
            flops=2 * row_count * depth * count * TILE,
            bytes_accessed=2 * depth * count * TILE,
            transcendentals=0,
        ),
        name="project",
    )(place, rows, pltpu.with_memory_space_constraint(weight, pltpu.HBM), *(pltpu.with_memory_space_constraint(w, pltpu.VMEM) for w in lead))


def shards(residual, query, new_keyval, key_cache, value_cache, lengths, out_weight):
    gx_count = lax.axis_size("gx")
    gx_index = lax.axis_index("gx")
    row_count = lengths.shape[0]
    query_width = query.shape[1]

    both = jnp.concatenate([query, new_keyval], axis=1).reshape(-1, row_count, query_width + new_keyval.shape[1])
    both = lax.all_to_all(both, ("gx", "gy"), split_axis=0, concat_axis=0, tiled=True)
    both = both.transpose(1, 0, 2)
    query_rows = both[:, :, :query_width].reshape(row_count, HEADS, HD)
    keyval_rows = both[:, :, query_width:].reshape(row_count, 2 * KV_HEADS, HD)

    frequency = ROPE_BASE ** (-2.0 * np.arange(HD // 2) / HD)
    frequency = np.concatenate([frequency, frequency]).astype(np.float32)
    side = np.where(np.arange(HD) < HD // 2, -1.0, 1.0).astype(np.float32)
    angles = lengths.astype(jnp.float32)[:, None] * frequency[None, :]
    turn = jnp.stack([jnp.cos(angles), jnp.sin(angles) * side], axis=1)

    bounded = jnp.minimum(lengths, key_cache.shape[1] - 1)
    near_place = jnp.reshape(gx_index % NEAR, (1,)).astype(jnp.int32)
    far_place = gx_index // NEAR
    far_count = gx_count // NEAR
    core = jnp.reshape(lax.axis_index("gy"), (1,)).astype(jnp.int32)
    bounded, near_place, far_place, core = lax.optimization_barrier((bounded, near_place, far_place, core))
    tiles = out_weight.shape[1] // TILE
    counts = [int(round(tiles * share)) for share in CHUNKS]
    mixed, lead = attention(
        bounded, query_rows, keyval_rows, turn, key_cache, value_cache, out_weight, tiles - counts[-1], gx_count
    )
    mixed, near_place, far_place, core = lax.optimization_barrier((mixed, near_place, far_place, core))
    mixed = lax.all_to_all(mixed, "gx", split_axis=0, concat_axis=0, tiled=True)
    other = lax.ppermute(mixed, "gy", [(0, 1), (1, 0)])
    feature_rows = arrangement(core, mixed, other)
    block_rows = feature_rows.shape[0] // gx_count
    starts = [sum(counts[:i]) for i in range(len(counts))]
    outs = []
    earlier = None
    leads = [lead]
    for first, count in reversed(list(zip(starts, counts))):
        columns = slice(first * TILE, (first + count) * TILE)
        own, *sends = projection(near_place, feature_rows, out_weight, leads, first, count, gx_count)
        leads = []
        if earlier is not None:
            own, earlier = lax.optimization_barrier((own, earlier))
        total = own
        for step, send in enumerate(sends, 1):
            got = lax.ppermute(send, "gx", [(i, i ^ step) for i in range(gx_count)])
            total = total + got.astype(jnp.float32)
        total = total.reshape(far_count, block_rows, count * TILE)
        if far_count == 2:
            low, high = total[0], total[1]
            mine = jnp.where(far_place == 0, low, high)
            send = jnp.where(far_place == 0, high, low).astype(jnp.bfloat16)
            got = lax.ppermute(send, "gx", [(i, i ^ NEAR) for i in range(gx_count)])
            earlier = got
            summed = mine + got.astype(jnp.float32)
        elif far_count > 1:
            parts = [[near + NEAR * far for far in range(far_count)] for near in range(NEAR)]
            got = lax.all_to_all(
                total.astype(jnp.bfloat16), "gx", split_axis=0, concat_axis=0,
                axis_index_groups=parts, tiled=True,
            )
            summed = jnp.sum(got.astype(jnp.float32), axis=0)
        else:
            summed = total[0]
        outs.append((residual[:, columns].astype(jnp.float32) + summed).astype(jnp.bfloat16))
    return jnp.concatenate(outs[::-1], axis=1)


def solution(mesh):
    in_specs = (
        P(("groups", "gx"), "gy"),
        P("groups", ("gx", "gy")),
        P("groups", ("gx", "gy")),
        P(("groups", "gx", "gy"), None, None),
        P(("groups", "gx", "gy"), None, None),
        P(("groups", "gx", "gy")),
        P("gx", "gy"),
    )
    out_specs = P(("groups", "gx"), "gy")
    return jax.shard_map(shards, mesh=mesh, in_specs=in_specs, out_specs=out_specs, check_vma=False)
```

time: 72.2 us -> 65.3 us (0.904)
  waiting for transfers between devices: 25.1 us -> 16.9 us
  blocking collectives: 1.98 us -> 9.74 us
  Pallas kernels: 21.8 us -> 17.6 us
  starting transfers between devices: 18.4 us -> 16.3 us
    all_to_all x0 -> x1, blocking collectives: none -> 9.74 us  [shards(): mixed = lax.all_to_all(mixed, 'gx', split_axis=0, concat_axis=0, tiled=True)]
    all_to_all x1 -> x0, waiting for transfers between devices: 7.27 us -> none  [shards(): mixed = lax.all_to_all(mixed, 'gx', split_axis=0, concat_axis=0, tiled=True)]
    ppermute x6, waiting for transfers between devices: 6.08 us -> 0.02 us  [shards(): got = lax.ppermute(send, 'gx', [(i, i ^ step) for i in range(gx_count)])]
    pallas_call x3 -> x4, Pallas kernels: 21.8 us -> 17.6 us  [the longest x2 10.8 us: projection(): pl.pallas_call(functools.partial(project, first, leads), out_shape=shapes...]
    ppermute x2, waiting for transfers between devices: 5.14 us -> 8.89 us  [shards(): got = lax.ppermute(send, 'gx', [(i, i ^ NEAR) for i in range(gx_count)])]
    all_to_all x1 -> x0, starting transfers between devices: 3.38 us -> none  [shards(): mixed = lax.all_to_all(mixed, 'gx', split_axis=0, concat_axis=0, tiled=True)]
    all_gather x1 -> x0, blocking collectives: 1.98 us -> none  [shards(): mixed = lax.all_gather(mixed, 'gy', axis=1)]
    ppermute x0 -> x1, waiting for transfers between devices: none -> 1.35 us  [shards(): other = lax.ppermute(mixed, 'gy', [(0, 1), (1, 0)])]
  transfers between devices with their start and end apart: 10 -> 10, of which waited for: 6 -> 4; matrix products, arithmetic and copies ran while one was open for 2% -> 3% of each run, Pallas kernels for 9% -> 8%
where the time goes in v3:
time: 65.3 us; the launch traced here: 64.9 us
  Pallas kernels  17.6 us (27%)
  waiting for transfers between devices  16.9 us (26%)
  starting transfers between devices  16.3 us (25%)
  blocking collectives  9.74 us (15%)
  other arithmetic  3.29 us (5%)
  local copies, waits for them, and re-layouts  0.87 us (1%)
    pallas_call x2, Pallas kernels, projection(): pl.pallas_call(functools.partial(project, first, leads), out_shape=shapes...  10.8 us
    all_to_all x1, blocking collectives, shards(): mixed = lax.all_to_all(mixed, 'gx', split_axis=0, concat_axis=0, tiled=True)  9.74 us
    ppermute x2, waiting for transfers between devices, shards(): got = lax.ppermute(send, 'gx', [(i, i ^ NEAR) for i in range(gx_count)])  8.89 us
    all_to_all x1, starting transfers between devices, shards(): lax.all_to_all(both, ('gx', 'gy'), split_axis=0, concat_axis=0, tiled=True)  7.36 us
    ppermute x6, starting transfers between devices, shards(): got = lax.ppermute(send, 'gx', [(i, i ^ step) for i in range(gx_count)])  7.11 us
    all_to_all x1, waiting for transfers between devices, shards(): lax.all_to_all(both, ('gx', 'gy'), split_axis=0, concat_axis=0, tiled=True)  6.61 us
    pallas_call x1, Pallas kernels, attention(): pl.pallas_call(functools.partial(attend, first), out_shape=(jax.ShapeDtyp...  6.6 us
    ppermute x2, starting transfers between devices, shards(): got = lax.ppermute(send, 'gx', [(i, i ^ NEAR) for i in range(gx_count)])  1.84 us
  transfers between devices with their start and end apart: 10, of which 4 were waited for; matrix products, arithmetic and copies ran while one was open for 3% of the time, Pallas kernels for 8%

profile of v3, /device:TPU:0, one launch (start us, length us, event | category | flops | bytes accessed | tf_op | source)
XLA Modules:
  0.0 64.9 jit_solution(36231899865726354)
XLA Ops:
  0.0 0.9 %pad_maximum_fusion = bf16[64,1152]{1,0:T(8,128)(2,1)S(1)} fusion(bf16[64,128]{1,0:T(8,128)(2,1)} %param.11, bf16[64,1024]{1,0:T(8,128)(2,1)} %param.10), kind=kLoop, calls=%fused_computation.4 | loop fusion | flops 294912 | bytes 294912 | tf_op jit(solution)/shard_map/concatenate | solution.py:235
  0.9 0.7 %reshape.136 = bf16[16,4,1152]{2,1,0:T(4,128)(2,1)} reshape(bf16[64,1152]{1,0:T(8,128)(2,1)S(1)} %pad_maximum_fusion) | data formatting | bytes 294912 | tf_op jit(solution)/shard_map/reshape | solution.py:235
  1.6 7.4 %all-to-all-start = ((bf16[16,4,1152]{2,1,0:T(4,128)(2,1)}), bf16[16,4,1152]{2,1,0:T(4,128)(2,1)S(1)}, u32[]{:S(2)}, u32[]{:S(2)}) async-start(bf16[16,4,1152]{2,1,0:T(4,128)(2,1)} %reshape.136), calls=%async_computation | async-start | bytes 294912 | tf_op jit(solution)/shard_map/all_to_all | solution.py:236
  9.0 0.7 %fusion = (f32[4]{0:T(128)S(1)}, s32[4]{0:T(128)S(1)}) fusion(s32[4]{0:T(128)} %param.14), kind=kLoop, calls=%fused_computation.13 | loop fusion | flops 8 | bytes 48 | tf_op jit(solution)/shard_map/convert_element_type | solution.py:244
  9.8 0.1 mul.39
  9.8 0.7 %multiply_cosine_fusion = (f32[4,1,128]{2,1,0:T(1,128)S(1)}, f32[4,1,128]{2,1,0:T(1,128)S(1)}) fusion(f32[4,1,128]{2,1,0:T(1,128)S(1)} %bitcast.8, f32[128]{0:T(128)} %constant.47, f32[128]{0:T(128)} %constant.42.clone), kind=kLoop, calls=%fused_computation.11 | loop fusion | flops 1024 | bytes 7168 | tf_op jit(solution)/shard_map/cos | solution.py:245
  10.6 6.6 %all-to-all-done = bf16[16,4,1152]{2,1,0:T(4,128)(2,1)S(1)} async-done(((bf16[16,4,1152]{2,1,0:T(4,128)(2,1)}), bf16[16,4,1152]{2,1,0:T(4,128)(2,1)S(1)}, u32[]{:S(2)}, u32[]{:S(2)}) %all-to-all-start) | async-done | bytes 147488 | tf_op jit(solution)/shard_map/all_to_all | solution.py:236
  17.3 0.1 reshape.137.query_ref
  17.3 6.6 %attend.1 = (bf16[8,4,16,128]{3,2,1,0:T(8,128)(2,1)S(1)}, bf16[4,2048,512]{2,1,0:T(8,128)(2,1)S(1)}) custom-call(s32[4]{0:T(128)S(1)} %get-tuple-element.24.lengths_ref, bf16[4,128,128]{2,1,0:T(8,128)(2,1)S(1)} %reshape.137.query_ref, bf16[4,16,128]{2,1,0:T(8,128)(2,1)S(1)} %slice.37.keyval_ref, f32[4,2,128]{2,1,0:T(2,128)S(1)} %pad_maximum_fusion.2.turn_ref, ...), custom_call_target="tpu_custom_call" | custom-call | flops 134217728 | bytes 8388608 | tf_op jit(solution)/shard_map/attend/pallas_call | solution.py:123
  23.9 9.7 %all_to_all.10.mine_ref = bf16[8,4,16,128]{3,2,1,0:T(8,128)(2,1)S(1)} all-to-all(bf16[8,4,16,128]{3,2,1,0:T(8,128)(2,1)S(1)} %get-tuple-element.32), channel_id=1, replica_groups=mesh['groups'=2,'gx'=8,'gy'=2] {'gx'}, dimensions={0} | all-to-all | bytes 262144 | tf_op jit(solution)/shard_map/all_to_all | solution.py:259
  33.7 0.0 collective-permute-start
  33.7 1.3 %collective-permute-done.other_ref = bf16[8,4,16,128]{3,2,1,0:T(8,128)(2,1)S(1)} collective-permute-done((bf16[8,4,16,128]{3,2,1,0:T(8,128)(2,1)S(1)}, bf16[8,4,16,128]{3,2,1,0:T(8,128)(2,1)S(1)}, u32[]{:S(2)}, u32[]{:S(2)}) %collective-permute-start) | collective-permute-done | bytes 131104 | tf_op jit(solution)/shard_map/ppermute | solution.py:260
  35.0 0.2 arrange.1.rows_ref
  35.2 5.5 %project.3 = (f32[16,5120]{1,0:T(8,128)S(1)}, bf16[16,5120]{1,0:T(8,128)(2,1)S(1)}, bf16[16,5120]{1,0:T(8,128)(2,1)S(1)}, bf16[16,5120]{1,0:T(8,128)(2,1)S(1)}) custom-call(s32[1]{0:T(128)} %bitcast.place_ref, bf16[64,2048]{1,0:T(8,128)(2,1)S(1)} %arrange.1.rows_ref, bf16[2048,8192]{1,0:T(8,128)(2,1)} %weight_hbm.5, ...), custom_call_target="tpu_custom_call" | custom-call | flops 1342177280 | bytes 20971520 | tf_op jit(solution)/shard_map/project/pallas_call | solution.py:209
  40.8 0.3 collective-permute-start.1
  41.0 1.1 %collective-permute-start.2 = (bf16[16,5120]{1,0:T(8,128)(2,1)S(1)}, bf16[16,5120]{1,0:T(8,128)(2,1)S(1)}, u32[]{:S(2)}, u32[]{:S(2)}) collective-permute-start(bf16[16,5120]{1,0:T(8,128)(2,1)S(1)} %get-tuple-element.37), channel_id=1, source_target_pairs={{0,4},{2,6},{4,0},{6,2},{8,12},{10,14},{12,8},{14,10},{1,5},{3,7},... | collective-permute-start | bytes 491528 | tf_op jit(solution)/shard_map/ppermute | solution.py:275
  42.1 2.2 %collective-permute-start.3 = (bf16[16,5120]{1,0:T(8,128)(2,1)S(1)}, bf16[16,5120]{1,0:T(8,128)(2,1)S(1)}, u32[]{:S(2)}, u32[]{:S(2)}) collective-permute-start(bf16[16,5120]{1,0:T(8,128)(2,1)S(1)} %get-tuple-element.38), channel_id=1, source_target_pairs={{0,6},{2,4},{4,2},{6,0},{8,14},{10,12},{12,10},{14,8},{1,7},{3,5},... | collective-permute-start | bytes 491528 | tf_op jit(solution)/shard_map/ppermute | solution.py:275
  44.3 0.0 copy-start
  44.3 5.3 %project.2 = (f32[16,3072]{1,0:T(8,128)S(1)}, bf16[16,3072]{1,0:T(8,128)(2,1)S(1)}, bf16[16,3072]{1,0:T(8,128)(2,1)S(1)}, bf16[16,3072]{1,0:T(8,128)(2,1)S(1)}) custom-call(s32[1]{0:T(128)} %bitcast.place_ref, bf16[64,2048]{1,0:T(8,128)(2,1)S(1)} %arrange.1.rows_ref, bf16[2048,8192]{1,0:T(8,128)(2,1)} %weight_hbm.5), custom_call_target="tpu_custom_call" | custom-call | flops 805306368 | bytes 12582912 | tf_op jit(solution)/shard_map/project/pallas_call | solution.py:209
  49.6 0.3 collective-permute-start.5
  49.9 1.1 %collective-permute-start.6 = (bf16[16,3072]{1,0:T(8,128)(2,1)S(1)}, bf16[16,3072]{1,0:T(8,128)(2,1)S(1)}, u32[]{:S(2)}, u32[]{:S(2)}) collective-permute-start(bf16[16,3072]{1,0:T(8,128)(2,1)S(1)} %get-tuple-element.41), channel_id=1, source_target_pairs={{0,4},{2,6},{4,0},{6,2},{8,12},{10,14},{12,8},{14,10},{1,5},{3,7},... | collective-permute-start | bytes 294920 | tf_op jit(solution)/shard_map/ppermute | solution.py:275
  51.0 0.0 collective-permute-done.1
  51.0 2.2 %collective-permute-start.7 = (bf16[16,3072]{1,0:T(8,128)(2,1)S(1)}, bf16[16,3072]{1,0:T(8,128)(2,1)S(1)}, u32[]{:S(2)}, u32[]{:S(2)}) collective-permute-start(bf16[16,3072]{1,0:T(8,128)(2,1)S(1)} %get-tuple-element.42), channel_id=1, source_target_pairs={{0,6},{2,4},{4,2},{6,0},{8,14},{10,12},{12,10},{14,8},{1,7},{3,5},... | collective-permute-start | bytes 294920 | tf_op jit(solution)/shard_map/ppermute | solution.py:275
  53.2 0.0 collective-permute-done.2
  53.2 0.0 collective-permute-done.3
  53.2 0.1 convert_add_fusion
  53.3 0.5 collective-permute-start.4
  53.7 5.3 %collective-permute-done.4 = bf16[8,5120]{1,0:T(8,128)(2,1)S(1)} collective-permute-done((bf16[8,5120]{1,0:T(8,128)(2,1)S(1)}, bf16[8,5120]{1,0:T(8,128)(2,1)S(1)}, u32[]{:S(2)}, u32[]{:S(2)}) %collective-permute-start.4) | collective-permute-done | bytes 81952 | tf_op jit(solution)/shard_map/ppermute | solution.py:282
  59.0 0.0 collective-permute-done.5
  59.0 0.0 collective-permute-done.6
  59.0 0.0 collective-permute-done.7
  59.1 1.4 %collective-permute-start.8 = (bf16[8,3072]{1,0:T(8,128)(2,1)S(1)}, bf16[8,3072]{1,0:T(8,128)(2,1)S(1)}, u32[]{:S(2)}, u32[]{:S(2)}) collective-permute-start(bf16[8,3072]{1,0:T(8,128)(2,1)S(1)} %select_convert_fusion.1), channel_id=1, source_target_pairs={{0,8},{2,10},{4,12},{6,14},{8,0},{10,2},{12,4},{14,6},{1,9},{3,11}... | collective-permute-start | bytes 147464 | tf_op jit(solution)/shard_map/ppermute | solution.py:282
  60.5 0.0 copy-done
  60.5 3.6 %collective-permute-done.8 = bf16[8,3072]{1,0:T(8,128)(2,1)S(1)} collective-permute-done((bf16[8,3072]{1,0:T(8,128)(2,1)S(1)}, bf16[8,3072]{1,0:T(8,128)(2,1)S(1)}, u32[]{:S(2)}, u32[]{:S(2)}) %collective-permute-start.8) | collective-permute-done | bytes 49184 | tf_op jit(solution)/shard_map/ppermute | solution.py:282
  64.2 0.7 %pad_maximum_fusion.1 = bf16[8,8192]{1,0:T(8,128)(2,1)} fusion(bf16[8,5120]{1,0:T(8,128)(2,1)S(1)} %add_convert_fusion, bf16[8,3072]{1,0:T(8,128)(2,1)S(1)} %add_convert_fusion.1), kind=kLoop, calls=%fused_computation.6 | loop fusion | flops 262144 | bytes 262144 | tf_op jit(solution)/shard_map/concatenate | solution.py:295
  (9 shorter events, 0.2 us)
Async XLA Ops:
  1.6 15.6 %all-to-all-start = ((bf16[16,4,1152]{2,1,0:T(4,128)(2,1)}), bf16[16,4,1152]{2,1,0:T(4,128)(2,1)S(1)}, u32[]{:S(2)}, u32[]{:S(2)}) async-start(bf16[16,4,1152]{2,1,0:T(4,128)(2,1)} %reshape.136), calls=%async_computation | async-start | bytes 294912 | tf_op jit(solution)/shard_map/all_to_all | solution.py:236
  33.7 1.3 %collective-permute-start = (bf16[8,4,16,128]{3,2,1,0:T(8,128)(2,1)S(1)}, bf16[8,4,16,128]{3,2,1,0:T(8,128)(2,1)S(1)}, u32[]{:S(2)}, u32[]{:S(2)}) collective-permute-start(bf16[8,4,16,128]{3,2,1,0:T(8,128)(2,1)S(1)} %all_to_all.10.mine_ref), channel_id=1, source_target_pairs={{0,1},{1,0},{2,3},{3,2},{4,5},{5,4},{6,7},{7,6},{8,9},{9,8},{10,11... | collective-permute-start | bytes 393224 | tf_op jit(solution)/shard_map/ppermute | solution.py:260
  40.8 10.3 %collective-permute-start.1 = (bf16[16,5120]{1,0:T(8,128)(2,1)S(1)}, bf16[16,5120]{1,0:T(8,128)(2,1)S(1)}, u32[]{:S(2)}, u32[]{:S(2)}) collective-permute-start(bf16[16,5120]{1,0:T(8,128)(2,1)S(1)} %get-tuple-element.36), channel_id=1, source_target_pairs={{0,2},{2,0},{4,6},{6,4},{8,10},{10,8},{12,14},{14,12},{1,3},{3,1},... | collective-permute-start | bytes 491528 | tf_op jit(solution)/shard_map/ppermute | solution.py:275
  41.0 12.1 %collective-permute-start.2 = (bf16[16,5120]{1,0:T(8,128)(2,1)S(1)}, bf16[16,5120]{1,0:T(8,128)(2,1)S(1)}, u32[]{:S(2)}, u32[]{:S(2)}) collective-permute-start(bf16[16,5120]{1,0:T(8,128)(2,1)S(1)} %get-tuple-element.37), channel_id=1, source_target_pairs={{0,4},{2,6},{4,0},{6,2},{8,12},{10,14},{12,8},{14,10},{1,5},{3,7},... | collective-permute-start | bytes 491528 | tf_op jit(solution)/shard_map/ppermute | solution.py:275
  42.1 11.1 %collective-permute-start.3 = (bf16[16,5120]{1,0:T(8,128)(2,1)S(1)}, bf16[16,5120]{1,0:T(8,128)(2,1)S(1)}, u32[]{:S(2)}, u32[]{:S(2)}) collective-permute-start(bf16[16,5120]{1,0:T(8,128)(2,1)S(1)} %get-tuple-element.38), channel_id=1, source_target_pairs={{0,6},{2,4},{4,2},{6,0},{8,14},{10,12},{12,10},{14,8},{1,7},{3,5},... | collective-permute-start | bytes 491528 | tf_op jit(solution)/shard_map/ppermute | solution.py:275
  44.3 16.2 %copy-start = (bf16[8,8192]{1,0:T(8,128)(2,1)S(1)}, bf16[8,8192]{1,0:T(8,128)(2,1)}, u32[]{:S(2)}) copy-start(bf16[8,8192]{1,0:T(8,128)(2,1)} %param.9) | copy-start | bytes 393220
  49.6 9.4 %collective-permute-start.5 = (bf16[16,3072]{1,0:T(8,128)(2,1)S(1)}, bf16[16,3072]{1,0:T(8,128)(2,1)S(1)}, u32[]{:S(2)}, u32[]{:S(2)}) collective-permute-start(bf16[16,3072]{1,0:T(8,128)(2,1)S(1)} %get-tuple-element.40), channel_id=1, source_target_pairs={{0,2},{2,0},{4,6},{6,4},{8,10},{10,8},{12,14},{14,12},{1,3},{3,1},... | collective-permute-start | bytes 294920 | tf_op jit(solution)/shard_map/ppermute | solution.py:275
  49.9 9.1 %collective-permute-start.6 = (bf16[16,3072]{1,0:T(8,128)(2,1)S(1)}, bf16[16,3072]{1,0:T(8,128)(2,1)S(1)}, u32[]{:S(2)}, u32[]{:S(2)}) collective-permute-start(bf16[16,3072]{1,0:T(8,128)(2,1)S(1)} %get-tuple-element.41), channel_id=1, source_target_pairs={{0,4},{2,6},{4,0},{6,2},{8,12},{10,14},{12,8},{14,10},{1,5},{3,7},... | collective-permute-start | bytes 294920 | tf_op jit(solution)/shard_map/ppermute | solution.py:275
  51.0 8.0 %collective-permute-start.7 = (bf16[16,3072]{1,0:T(8,128)(2,1)S(1)}, bf16[16,3072]{1,0:T(8,128)(2,1)S(1)}, u32[]{:S(2)}, u32[]{:S(2)}) collective-permute-start(bf16[16,3072]{1,0:T(8,128)(2,1)S(1)} %get-tuple-element.42), channel_id=1, source_target_pairs={{0,6},{2,4},{4,2},{6,0},{8,14},{10,12},{12,10},{14,8},{1,7},{3,5},... | collective-permute-start | bytes 294920 | tf_op jit(solution)/shard_map/ppermute | solution.py:275
  53.3 5.7 %collective-permute-start.4 = (bf16[8,5120]{1,0:T(8,128)(2,1)S(1)}, bf16[8,5120]{1,0:T(8,128)(2,1)S(1)}, u32[]{:S(2)}, u32[]{:S(2)}) collective-permute-start(bf16[8,5120]{1,0:T(8,128)(2,1)S(1)} %select_convert_fusion), channel_id=1, source_target_pairs={{0,8},{2,10},{4,12},{6,14},{8,0},{10,2},{12,4},{14,6},{1,9},{3,11}... | collective-permute-start | bytes 245768 | tf_op jit(solution)/shard_map/ppermute | solution.py:282
  59.1 5.1 %collective-permute-start.8 = (bf16[8,3072]{1,0:T(8,128)(2,1)S(1)}, bf16[8,3072]{1,0:T(8,128)(2,1)S(1)}, u32[]{:S(2)}, u32[]{:S(2)}) collective-permute-start(bf16[8,3072]{1,0:T(8,128)(2,1)S(1)} %select_convert_fusion.1), channel_id=1, source_target_pairs={{0,8},{2,10},{4,12},{6,14},{8,0},{10,2},{12,4},{14,6},{1,9},{3,11}... | collective-permute-start | bytes 147464 | tf_op jit(solution)/shard_map/ppermute | solution.py:282

commit v4 on v3

--- a/solution.py
+++ b/solution.py
@@ -271,7 +271,8 @@
         if earlier is not None:
             own, earlier = lax.optimization_barrier((own, earlier))
         total = own
-        for step, send in enumerate(sends, 1):
+        for step in (3, 1, 2):
+            send = sends[step - 1]
             got = lax.ppermute(send, "gx", [(i, i ^ step) for i in range(gx_count)])
             total = total + got.astype(jnp.float32)
         total = total.reshape(far_count, block_rows, count * TILE)

time: 65.3 us -> 65.3 us (level)
  no operation moved by 1% of the time
where the time goes in v4:
time: 65.3 us; the launch traced here: 64.9 us
  Pallas kernels  17.6 us (27%)
  waiting for transfers between devices  17.4 us (27%)
  starting transfers between devices  15.8 us (24%)
  blocking collectives  9.74 us (15%)
  other arithmetic  3.31 us (5%)
  local copies, waits for them, and re-layouts  0.87 us (1%)
    pallas_call x2, Pallas kernels, projection(): pl.pallas_call(functools.partial(project, first, leads), out_shape=shapes...  10.8 us
    all_to_all x1, blocking collectives, shards(): mixed = lax.all_to_all(mixed, 'gx', split_axis=0, concat_axis=0, tiled=True)  9.74 us
    ppermute x2, waiting for transfers between devices, shards(): got = lax.ppermute(send, 'gx', [(i, i ^ NEAR) for i in range(gx_count)])  9.44 us
    all_to_all x1, starting transfers between devices, shards(): lax.all_to_all(both, ('gx', 'gy'), split_axis=0, concat_axis=0, tiled=True)  7.36 us
    ppermute x6, starting transfers between devices, shards(): got = lax.ppermute(send, 'gx', [(i, i ^ step) for i in range(gx_count)])  7.11 us
    all_to_all x1, waiting for transfers between devices, shards(): lax.all_to_all(both, ('gx', 'gy'), split_axis=0, concat_axis=0, tiled=True)  6.61 us
    pallas_call x1, Pallas kernels, attention(): pl.pallas_call(functools.partial(attend, first), out_shape=(jax.ShapeDtyp...  6.6 us
    ppermute x1, waiting for transfers between devices, shards(): other = lax.ppermute(mixed, 'gy', [(0, 1), (1, 0)])  1.35 us
  transfers between devices with their start and end apart: 10, of which 4 were waited for; matrix products, arithmetic and copies ran while one was open for 3% of the time, Pallas kernels for 8%

profile of v4, /device:TPU:0, one launch (start us, length us, event | category | flops | bytes accessed | tf_op | source)
XLA Modules:
  0.0 64.9 jit_solution(14270003277396691644)
XLA Ops:
  0.0 0.9 %pad_maximum_fusion = bf16[64,1152]{1,0:T(8,128)(2,1)S(1)} fusion(bf16[64,128]{1,0:T(8,128)(2,1)} %param.11, bf16[64,1024]{1,0:T(8,128)(2,1)} %param.10), kind=kLoop, calls=%fused_computation.4 | loop fusion | flops 294912 | bytes 294912 | tf_op jit(solution)/shard_map/concatenate | solution.py:235
  0.9 0.7 %reshape.136 = bf16[16,4,1152]{2,1,0:T(4,128)(2,1)} reshape(bf16[64,1152]{1,0:T(8,128)(2,1)S(1)} %pad_maximum_fusion) | data formatting | bytes 294912 | tf_op jit(solution)/shard_map/reshape | solution.py:235
  1.6 7.4 %all-to-all-start = ((bf16[16,4,1152]{2,1,0:T(4,128)(2,1)}), bf16[16,4,1152]{2,1,0:T(4,128)(2,1)S(1)}, u32[]{:S(2)}, u32[]{:S(2)}) async-start(bf16[16,4,1152]{2,1,0:T(4,128)(2,1)} %reshape.136), calls=%async_computation | async-start | bytes 294912 | tf_op jit(solution)/shard_map/all_to_all | solution.py:236
  9.0 0.7 %fusion = (f32[4]{0:T(128)S(1)}, s32[4]{0:T(128)S(1)}) fusion(s32[4]{0:T(128)} %param.14), kind=kLoop, calls=%fused_computation.13 | loop fusion | flops 8 | bytes 48 | tf_op jit(solution)/shard_map/convert_element_type | solution.py:244
  9.8 0.1 mul.39
  9.8 0.7 %multiply_cosine_fusion = (f32[4,1,128]{2,1,0:T(1,128)S(1)}, f32[4,1,128]{2,1,0:T(1,128)S(1)}) fusion(f32[4,1,128]{2,1,0:T(1,128)S(1)} %bitcast.8, f32[128]{0:T(128)} %constant.47, f32[128]{0:T(128)} %constant.42.clone), kind=kLoop, calls=%fused_computation.11 | loop fusion | flops 1024 | bytes 7168 | tf_op jit(solution)/shard_map/cos | solution.py:245
  10.6 6.6 %all-to-all-done = bf16[16,4,1152]{2,1,0:T(4,128)(2,1)S(1)} async-done(((bf16[16,4,1152]{2,1,0:T(4,128)(2,1)}), bf16[16,4,1152]{2,1,0:T(4,128)(2,1)S(1)}, u32[]{:S(2)}, u32[]{:S(2)}) %all-to-all-start) | async-done | bytes 147488 | tf_op jit(solution)/shard_map/all_to_all | solution.py:236
  17.3 0.1 reshape.137.query_ref
  17.3 6.6 %attend.1 = (bf16[8,4,16,128]{3,2,1,0:T(8,128)(2,1)S(1)}, bf16[4,2048,512]{2,1,0:T(8,128)(2,1)S(1)}) custom-call(s32[4]{0:T(128)S(1)} %get-tuple-element.24.lengths_ref, bf16[4,128,128]{2,1,0:T(8,128)(2,1)S(1)} %reshape.137.query_ref, bf16[4,16,128]{2,1,0:T(8,128)(2,1)S(1)} %slice.37.keyval_ref, f32[4,2,128]{2,1,0:T(2,128)S(1)} %pad_maximum_fusion.2.turn_ref, ...), custom_call_target="tpu_custom_call" | custom-call | flops 134217728 | bytes 8388608 | tf_op jit(solution)/shard_map/attend/pallas_call | solution.py:123
  23.9 9.7 %all_to_all.10.mine_ref = bf16[8,4,16,128]{3,2,1,0:T(8,128)(2,1)S(1)} all-to-all(bf16[8,4,16,128]{3,2,1,0:T(8,128)(2,1)S(1)} %get-tuple-element.32), channel_id=1, replica_groups=mesh['groups'=2,'gx'=8,'gy'=2] {'gx'}, dimensions={0} | all-to-all | bytes 262144 | tf_op jit(solution)/shard_map/all_to_all | solution.py:259
  33.7 0.0 collective-permute-start
  33.7 1.3 %collective-permute-done.other_ref = bf16[8,4,16,128]{3,2,1,0:T(8,128)(2,1)S(1)} collective-permute-done((bf16[8,4,16,128]{3,2,1,0:T(8,128)(2,1)S(1)}, bf16[8,4,16,128]{3,2,1,0:T(8,128)(2,1)S(1)}, u32[]{:S(2)}, u32[]{:S(2)}) %collective-permute-start) | collective-permute-done | bytes 131104 | tf_op jit(solution)/shard_map/ppermute | solution.py:260
  35.0 0.2 arrange.1.rows_ref
  35.2 5.5 %project.3 = (f32[16,5120]{1,0:T(8,128)S(1)}, bf16[16,5120]{1,0:T(8,128)(2,1)S(1)}, bf16[16,5120]{1,0:T(8,128)(2,1)S(1)}, bf16[16,5120]{1,0:T(8,128)(2,1)S(1)}) custom-call(s32[1]{0:T(128)} %bitcast.place_ref, bf16[64,2048]{1,0:T(8,128)(2,1)S(1)} %arrange.1.rows_ref, bf16[2048,8192]{1,0:T(8,128)(2,1)} %weight_hbm.5, ...), custom_call_target="tpu_custom_call" | custom-call | flops 1342177280 | bytes 20971520 | tf_op jit(solution)/shard_map/project/pallas_call | solution.py:209
  40.8 0.8 %collective-permute-start.1 = (bf16[16,5120]{1,0:T(8,128)(2,1)S(1)}, bf16[16,5120]{1,0:T(8,128)(2,1)S(1)}, u32[]{:S(2)}, u32[]{:S(2)}) collective-permute-start(bf16[16,5120]{1,0:T(8,128)(2,1)S(1)} %get-tuple-element.36), channel_id=1, source_target_pairs={{0,6},{2,4},{4,2},{6,0},{8,14},{10,12},{12,10},{14,8},{1,7},{3,5},... | collective-permute-start | bytes 491528 | tf_op jit(solution)/shard_map/ppermute | solution.py:276
  41.6 0.6 collective-permute-start.2
  42.2 2.2 %collective-permute-start.3 = (bf16[16,5120]{1,0:T(8,128)(2,1)S(1)}, bf16[16,5120]{1,0:T(8,128)(2,1)S(1)}, u32[]{:S(2)}, u32[]{:S(2)}) collective-permute-start(bf16[16,5120]{1,0:T(8,128)(2,1)S(1)} %get-tuple-element.38), channel_id=1, source_target_pairs={{0,4},{2,6},{4,0},{6,2},{8,12},{10,14},{12,8},{14,10},{1,5},{3,7},... | collective-permute-start | bytes 491528 | tf_op jit(solution)/shard_map/ppermute | solution.py:276
  44.3 0.0 copy-start
  44.3 5.3 %project.2 = (f32[16,3072]{1,0:T(8,128)S(1)}, bf16[16,3072]{1,0:T(8,128)(2,1)S(1)}, bf16[16,3072]{1,0:T(8,128)(2,1)S(1)}, bf16[16,3072]{1,0:T(8,128)(2,1)S(1)}) custom-call(s32[1]{0:T(128)} %bitcast.place_ref, bf16[64,2048]{1,0:T(8,128)(2,1)S(1)} %arrange.1.rows_ref, bf16[2048,8192]{1,0:T(8,128)(2,1)} %weight_hbm.5), custom_call_target="tpu_custom_call" | custom-call | flops 805306368 | bytes 12582912 | tf_op jit(solution)/shard_map/project/pallas_call | solution.py:209
  49.6 0.8 %collective-permute-start.5 = (bf16[16,3072]{1,0:T(8,128)(2,1)S(1)}, bf16[16,3072]{1,0:T(8,128)(2,1)S(1)}, u32[]{:S(2)}, u32[]{:S(2)}) collective-permute-start(bf16[16,3072]{1,0:T(8,128)(2,1)S(1)} %get-tuple-element.40), channel_id=1, source_target_pairs={{0,6},{2,4},{4,2},{6,0},{8,14},{10,12},{12,10},{14,8},{1,7},{3,5},... | collective-permute-start | bytes 294920 | tf_op jit(solution)/shard_map/ppermute | solution.py:276
  50.4 0.7 %collective-permute-start.6 = (bf16[16,3072]{1,0:T(8,128)(2,1)S(1)}, bf16[16,3072]{1,0:T(8,128)(2,1)S(1)}, u32[]{:S(2)}, u32[]{:S(2)}) collective-permute-start(bf16[16,3072]{1,0:T(8,128)(2,1)S(1)} %get-tuple-element.41), channel_id=1, source_target_pairs={{0,2},{2,0},{4,6},{6,4},{8,10},{10,8},{12,14},{14,12},{1,3},{3,1},... | collective-permute-start | bytes 294920 | tf_op jit(solution)/shard_map/ppermute | solution.py:276
  51.2 0.0 collective-permute-done.1
  51.2 2.0 %collective-permute-start.7 = (bf16[16,3072]{1,0:T(8,128)(2,1)S(1)}, bf16[16,3072]{1,0:T(8,128)(2,1)S(1)}, u32[]{:S(2)}, u32[]{:S(2)}) collective-permute-start(bf16[16,3072]{1,0:T(8,128)(2,1)S(1)} %get-tuple-element.42), channel_id=1, source_target_pairs={{0,4},{2,6},{4,0},{6,2},{8,12},{10,14},{12,8},{14,10},{1,5},{3,7},... | collective-permute-start | bytes 294920 | tf_op jit(solution)/shard_map/ppermute | solution.py:276
  53.2 0.0 collective-permute-done.2
  53.2 0.0 collective-permute-done.3
  53.2 0.1 convert_add_fusion
  53.3 0.5 collective-permute-start.4
  53.7 5.3 %collective-permute-done.4 = bf16[8,5120]{1,0:T(8,128)(2,1)S(1)} collective-permute-done((bf16[8,5120]{1,0:T(8,128)(2,1)S(1)}, bf16[8,5120]{1,0:T(8,128)(2,1)S(1)}, u32[]{:S(2)}, u32[]{:S(2)}) %collective-permute-start.4) | collective-permute-done | bytes 81952 | tf_op jit(solution)/shard_map/ppermute | solution.py:283
  59.0 0.0 collective-permute-done.5
  59.0 0.0 collective-permute-done.6
  59.0 0.0 collective-permute-done.7
  59.1 0.9 %collective-permute-start.8 = (bf16[8,3072]{1,0:T(8,128)(2,1)S(1)}, bf16[8,3072]{1,0:T(8,128)(2,1)S(1)}, u32[]{:S(2)}, u32[]{:S(2)}) collective-permute-start(bf16[8,3072]{1,0:T(8,128)(2,1)S(1)} %select_convert_fusion.1), channel_id=1, source_target_pairs={{0,8},{2,10},{4,12},{6,14},{8,0},{10,2},{12,4},{14,6},{1,9},{3,11}... | collective-permute-start | bytes 147464 | tf_op jit(solution)/shard_map/ppermute | solution.py:283
  60.0 0.0 copy-done
  60.0 4.2 %collective-permute-done.8 = bf16[8,3072]{1,0:T(8,128)(2,1)S(1)} collective-permute-done((bf16[8,3072]{1,0:T(8,128)(2,1)S(1)}, bf16[8,3072]{1,0:T(8,128)(2,1)S(1)}, u32[]{:S(2)}, u32[]{:S(2)}) %collective-permute-start.8) | collective-permute-done | bytes 49184 | tf_op jit(solution)/shard_map/ppermute | solution.py:283
  64.2 0.7 %pad_maximum_fusion.1 = bf16[8,8192]{1,0:T(8,128)(2,1)} fusion(bf16[8,5120]{1,0:T(8,128)(2,1)S(1)} %add_convert_fusion, bf16[8,3072]{1,0:T(8,128)(2,1)S(1)} %add_convert_fusion.1), kind=kLoop, calls=%fused_computation.6 | loop fusion | flops 262144 | bytes 262144 | tf_op jit(solution)/shard_map/concatenate | solution.py:296
  (9 shorter events, 0.2 us)
Async XLA Ops:
  1.6 15.6 %all-to-all-start = ((bf16[16,4,1152]{2,1,0:T(4,128)(2,1)}), bf16[16,4,1152]{2,1,0:T(4,128)(2,1)S(1)}, u32[]{:S(2)}, u32[]{:S(2)}) async-start(bf16[16,4,1152]{2,1,0:T(4,128)(2,1)} %reshape.136), calls=%async_computation | async-start | bytes 294912 | tf_op jit(solution)/shard_map/all_to_all | solution.py:236
  33.7 1.3 %collective-permute-start = (bf16[8,4,16,128]{3,2,1,0:T(8,128)(2,1)S(1)}, bf16[8,4,16,128]{3,2,1,0:T(8,128)(2,1)S(1)}, u32[]{:S(2)}, u32[]{:S(2)}) collective-permute-start(bf16[8,4,16,128]{3,2,1,0:T(8,128)(2,1)S(1)} %all_to_all.10.mine_ref), channel_id=1, source_target_pairs={{0,1},{1,0},{2,3},{3,2},{4,5},{5,4},{6,7},{7,6},{8,9},{9,8},{10,11... | collective-permute-start | bytes 393224 | tf_op jit(solution)/shard_map/ppermute | solution.py:260
  40.8 10.4 %collective-permute-start.1 = (bf16[16,5120]{1,0:T(8,128)(2,1)S(1)}, bf16[16,5120]{1,0:T(8,128)(2,1)S(1)}, u32[]{:S(2)}, u32[]{:S(2)}) collective-permute-start(bf16[16,5120]{1,0:T(8,128)(2,1)S(1)} %get-tuple-element.36), channel_id=1, source_target_pairs={{0,6},{2,4},{4,2},{6,0},{8,14},{10,12},{12,10},{14,8},{1,7},{3,5},... | collective-permute-start | bytes 491528 | tf_op jit(solution)/shard_map/ppermute | solution.py:276
  41.6 11.6 %collective-permute-start.2 = (bf16[16,5120]{1,0:T(8,128)(2,1)S(1)}, bf16[16,5120]{1,0:T(8,128)(2,1)S(1)}, u32[]{:S(2)}, u32[]{:S(2)}) collective-permute-start(bf16[16,5120]{1,0:T(8,128)(2,1)S(1)} %get-tuple-element.37), channel_id=1, source_target_pairs={{0,2},{2,0},{4,6},{6,4},{8,10},{10,8},{12,14},{14,12},{1,3},{3,1},... | collective-permute-start | bytes 491528 | tf_op jit(solution)/shard_map/ppermute | solution.py:276
  42.2 11.0 %collective-permute-start.3 = (bf16[16,5120]{1,0:T(8,128)(2,1)S(1)}, bf16[16,5120]{1,0:T(8,128)(2,1)S(1)}, u32[]{:S(2)}, u32[]{:S(2)}) collective-permute-start(bf16[16,5120]{1,0:T(8,128)(2,1)S(1)} %get-tuple-element.38), channel_id=1, source_target_pairs={{0,4},{2,6},{4,0},{6,2},{8,12},{10,14},{12,8},{14,10},{1,5},{3,7},... | collective-permute-start | bytes 491528 | tf_op jit(solution)/shard_map/ppermute | solution.py:276
  44.3 15.7 %copy-start = (bf16[8,8192]{1,0:T(8,128)(2,1)S(1)}, bf16[8,8192]{1,0:T(8,128)(2,1)}, u32[]{:S(2)}) copy-start(bf16[8,8192]{1,0:T(8,128)(2,1)} %param.9) | copy-start | bytes 393220
  49.6 9.4 %collective-permute-start.5 = (bf16[16,3072]{1,0:T(8,128)(2,1)S(1)}, bf16[16,3072]{1,0:T(8,128)(2,1)S(1)}, u32[]{:S(2)}, u32[]{:S(2)}) collective-permute-start(bf16[16,3072]{1,0:T(8,128)(2,1)S(1)} %get-tuple-element.40), channel_id=1, source_target_pairs={{0,6},{2,4},{4,2},{6,0},{8,14},{10,12},{12,10},{14,8},{1,7},{3,5},... | collective-permute-start | bytes 294920 | tf_op jit(solution)/shard_map/ppermute | solution.py:276
  50.4 8.6 %collective-permute-start.6 = (bf16[16,3072]{1,0:T(8,128)(2,1)S(1)}, bf16[16,3072]{1,0:T(8,128)(2,1)S(1)}, u32[]{:S(2)}, u32[]{:S(2)}) collective-permute-start(bf16[16,3072]{1,0:T(8,128)(2,1)S(1)} %get-tuple-element.41), channel_id=1, source_target_pairs={{0,2},{2,0},{4,6},{6,4},{8,10},{10,8},{12,14},{14,12},{1,3},{3,1},... | collective-permute-start | bytes 294920 | tf_op jit(solution)/shard_map/ppermute | solution.py:276
  51.2 7.9 %collective-permute-start.7 = (bf16[16,3072]{1,0:T(8,128)(2,1)S(1)}, bf16[16,3072]{1,0:T(8,128)(2,1)S(1)}, u32[]{:S(2)}, u32[]{:S(2)}) collective-permute-start(bf16[16,3072]{1,0:T(8,128)(2,1)S(1)} %get-tuple-element.42), channel_id=1, source_target_pairs={{0,4},{2,6},{4,0},{6,2},{8,12},{10,14},{12,8},{14,10},{1,5},{3,7},... | collective-permute-start | bytes 294920 | tf_op jit(solution)/shard_map/ppermute | solution.py:276
  53.3 5.7 %collective-permute-start.4 = (bf16[8,5120]{1,0:T(8,128)(2,1)S(1)}, bf16[8,5120]{1,0:T(8,128)(2,1)S(1)}, u32[]{:S(2)}, u32[]{:S(2)}) collective-permute-start(bf16[8,5120]{1,0:T(8,128)(2,1)S(1)} %select_convert_fusion), channel_id=1, source_target_pairs={{0,8},{2,10},{4,12},{6,14},{8,0},{10,2},{12,4},{14,6},{1,9},{3,11}... | collective-permute-start | bytes 245768 | tf_op jit(solution)/shard_map/ppermute | solution.py:283
  59.1 5.1 %collective-permute-start.8 = (bf16[8,3072]{1,0:T(8,128)(2,1)S(1)}, bf16[8,3072]{1,0:T(8,128)(2,1)S(1)}, u32[]{:S(2)}, u32[]{:S(2)}) collective-permute-start(bf16[8,3072]{1,0:T(8,128)(2,1)S(1)} %select_convert_fusion.1), channel_id=1, source_target_pairs={{0,8},{2,10},{4,12},{6,14},{8,0},{10,2},{12,4},{14,6},{1,9},{3,11}... | collective-permute-start | bytes 147464 | tf_op jit(solution)/shard_map/ppermute | solution.py:283
